TPU v7x, 256 devices: a whole 4x4x8 slice. The times are simulated.
256 devices in a mesh: seq: 32 (over z, y_lo, core), tensor: 4 (over x), dp: 2 (over y_hi).
Axes of the slice: x: 4, y: 4 (y_hi: 2, y_lo: 2; y = y_hi * 2 + y_lo), z: 8, core: 2. Of those that a mesh axis runs over, the one named last changes fastest.
Arguments:
- queries: bfloat16 [2, 4096, 4096], P('dp', 'seq', 'tensor'), may hold values from -8 to 8
- neighbour_kv: bfloat16 [2, 16384, 2, 4096], P('dp', 'seq', None, 'tensor'), may hold values from -8 to 8
- block_target: int32 [2, 1024], P('dp', 'seq'), may hold values from 0 to 1023, as said below
- neighbour_count: int32 [2, 64], P('dp'), may hold values from 1 to 2
- out_weight: bfloat16 [32, 128, 4096], P('tensor', None, 'dp'), may hold values from -0.09375 to 0.09375
- grad_mixed: bfloat16 [2, 4096, 4096], P('dp', 'seq', 'tensor'), may hold values from -6 to 6
Outputs:
- layer_out: bfloat16 [2, 4096, 4096], P('dp', 'seq', 'tensor')
- grad_queries: bfloat16 [2, 4096, 4096], P('dp', 'seq', 'tensor')
- grad_kv: bfloat16 [2, 16384, 2, 4096], P('dp', 'seq', None, 'tensor')
- grad_out_weight: float32 [32, 128, 4096], P('tensor', 'seq', 'dp')
Inputs may be any that keep to these rules, and one draw needn't show every extreme that they name: `block_target`: for each replica the entries are a permutation; the 32 blocks of one device's rows name exactly one of the blocks (b * 32 to b * 32 + 31) of each seq index b.
All inputs are finite; a program needn't handle non-finite values.
Results may differ from a plain program's by a relative error of at most 0.035.
Values may be sent and summed in bfloat16 or wider, within the bound.
No kernel may reach another device: no remote copies, remote signals or barrier semaphores. Data moves between devices by JAX's collectives and lax.ppermute only.
A program may use at most 128 MiB of HBM per device.

v0:
```python
import jax
import jax.numpy as jnp
from jax import lax
from jax.sharding import PartitionSpec as P

CLEN = 64
NLEN = 128
NEIGH = 2


NEG_FILL = -1e30


def passed_along(value, axis, steps):
    count = lax.axis_size(axis)
    initial, last = (max(0, -steps), min(count, count - steps))
    return lax.ppermute(value, axis, [(source, source + steps) for source in range(initial, last)])


def attend_groups(query_groups, kv_groups, key_live, head_size):
    groups, span_len, inner_dev = query_groups.shape
    keys_len = kv_groups.shape[1]
    heads_dev = inner_dev // head_size
    score_scale = head_size ** (-0.5)
    query_heads = query_groups.reshape(groups, span_len, heads_dev, head_size)
    key_heads = kv_groups[:, :, 0].reshape(groups, keys_len, heads_dev, head_size)
    value_heads = kv_groups[:, :, 1].reshape(groups, keys_len, heads_dev, head_size)
    scores = (
        jnp.einsum("gqhd,gkhd->ghqk", query_heads, key_heads, preferred_element_type=jnp.float32)
        * score_scale
    )
    scores = jnp.where(key_live[:, None, None, :], scores, NEG_FILL)
    row_top = jnp.max(scores, axis=-1, keepdims=True)
    raw_weights = jnp.exp(scores - row_top)
    soft_weights = raw_weights / jnp.sum(raw_weights, axis=-1, keepdims=True)
    low_weights = soft_weights.astype(jnp.bfloat16)
    context = jnp.einsum(
        "ghqk,gkhd->gqhd", low_weights, value_heads, preferred_element_type=jnp.float32
    )
    return (
        context.reshape(groups, span_len, inner_dev).astype(jnp.bfloat16),
        soft_weights,
        low_weights,
    )


def attend_back(
    query_groups, kv_groups, soft_weights, low_weights, context, grad_context, head_size
):
    groups, span_len, inner_dev = query_groups.shape
    keys_len = kv_groups.shape[1]
    heads_dev = inner_dev // head_size
    score_scale = head_size ** (-0.5)
    query_heads = query_groups.reshape(groups, span_len, heads_dev, head_size)
    key_heads = kv_groups[:, :, 0].reshape(groups, keys_len, heads_dev, head_size)
    value_heads = kv_groups[:, :, 1].reshape(groups, keys_len, heads_dev, head_size)
    grad_heads = grad_context.reshape(groups, span_len, heads_dev, head_size)
    grad_value = jnp.einsum(
        "ghqk,gqhd->gkhd", low_weights, grad_heads, preferred_element_type=jnp.float32
    )
    grad_weights = jnp.einsum(
        "gqhd,gkhd->ghqk", grad_heads, value_heads, preferred_element_type=jnp.float32
    )
    context_heads = context.reshape(groups, span_len, heads_dev, head_size).astype(jnp.float32)
    row_delta = jnp.sum(grad_heads.astype(jnp.float32) * context_heads, axis=-1)
    row_delta = jnp.transpose(row_delta, (0, 2, 1))[..., None]
    grad_scores = soft_weights * (grad_weights - row_delta)
    grad_query = (
        jnp.einsum(
            "ghqk,gkhd->gqhd",
            grad_scores,
            key_heads.astype(jnp.float32),
            precision=lax.Precision.HIGHEST,
            preferred_element_type=jnp.float32,
        )
        * score_scale
    )
    grad_key = (
        jnp.einsum(
            "ghqk,gqhd->gkhd",
            grad_scores,
            query_heads.astype(jnp.float32),
            precision=lax.Precision.HIGHEST,
            preferred_element_type=jnp.float32,
        )
        * score_scale
    )
    grad_pair = jnp.stack([grad_key, grad_value], axis=2).reshape(groups, keys_len, 2, inner_dev)
    return (grad_query.reshape(groups, span_len, inner_dev), grad_pair)


def local(queries, neighbour_kv, block_target, neighbour_count, out_weight, grad_mixed):
    shards = lax.axis_size("seq")
    seq_place = lax.axis_index("seq")
    query_rows = queries[0]
    token_count, inner_dev = query_rows.shape
    head_size = out_weight.shape[1]
    span_len = CLEN
    spans_dev = token_count // span_len
    keys_len = NEIGH * NLEN
    lead_len = span_len - 1
    local_kv = neighbour_kv[0]
    owner_rows = local_kv.shape[0]
    block_rows = owner_rows // shards
    blocks = local_kv.reshape(shards, block_rows, 2, inner_dev)
    target = block_target[0]
    destination = target // shards
    send_order = jnp.argsort(destination)
    outgoing = blocks[send_order]
    outgoing_target = target[send_order].reshape(shards, 1)
    incoming, incoming_target = (
        lax.all_to_all(outgoing, "seq", split_axis=0, concat_axis=0, tiled=True),
        lax.all_to_all(outgoing_target, "seq", split_axis=0, concat_axis=0, tiled=True),
    )
    local_slot = incoming_target[:, 0] % shards
    arranged = incoming[jnp.argsort(local_slot)].reshape(spans_dev, keys_len, 2, inner_dev)
    counts_all = neighbour_count[0]
    span_total = counts_all.shape[0]
    key_index = jnp.arange(keys_len)
    previous = passed_along(arranged[spans_dev - 1], "seq", 1)
    kv_groups = jnp.concatenate([previous[None], arranged], axis=0)
    group_spans = seq_place * spans_dev - 1 + jnp.arange(spans_dev + 1)
    live_scale = (group_spans >= 0).astype(jnp.bfloat16)[:, None, None]
    matches = group_spans[:, None] == jnp.arange(span_total)[None, :]
    key_live = (
        key_index[None, :]
        < jnp.sum(jnp.where(matches, counts_all[None, :], 0), axis=1)[:, None] * NLEN
    )
    query_groups = jnp.concatenate(
        [
            jnp.zeros((1, inner_dev), jnp.bfloat16),
            query_rows,
            jnp.zeros((lead_len, inner_dev), jnp.bfloat16),
        ],
        axis=0,
    )
    query_groups = query_groups.reshape(spans_dev + 1, span_len, inner_dev)
    context_groups, soft_weights, low_weights = attend_groups(
        query_groups, kv_groups, key_live, head_size
    )
    context_groups = context_groups * live_scale
    context = context_groups.reshape(-1, inner_dev)[1 : 1 + token_count]
    grad_full = lax.all_gather(grad_mixed[0], "tensor", axis=1, tiled=True)
    full_weight = lax.all_gather(out_weight, "dp", axis=2, tiled=True)
    weight_mat = full_weight.reshape(inner_dev, -1)
    partial_out = jnp.dot(context, weight_mat, preferred_element_type=jnp.float32)
    layer_out = lax.psum_scatter(partial_out, "tensor", scatter_dimension=1, tiled=True).astype(
        jnp.bfloat16
    )
    grad_context = lax.dot_general(
        grad_full, weight_mat, (((1,), (1,)), ((), ())), preferred_element_type=jnp.float32
    ).astype(jnp.bfloat16)
    weight_terms = lax.dot_general(
        context, grad_full, (((0,), (0,)), ((), ())), preferred_element_type=jnp.float32
    ).reshape(full_weight.shape)
    partial_grad = lax.psum_scatter(weight_terms, "seq", scatter_dimension=1, tiled=True)
    weight_grad = lax.psum_scatter(partial_grad, "dp", scatter_dimension=2, tiled=True)
    grad_groups = jnp.concatenate(
        [
            jnp.zeros((1, inner_dev), jnp.bfloat16),
            grad_context,
            jnp.zeros((lead_len, inner_dev), jnp.bfloat16),
        ],
        axis=0,
    )
    grad_groups = grad_groups.reshape(spans_dev + 1, span_len, inner_dev) * live_scale
    grad_query_groups, grad_kv_groups = attend_back(
        query_groups, kv_groups, soft_weights, low_weights, context_groups, grad_groups, head_size
    )
    grad_queries = grad_query_groups.reshape(-1, inner_dev)[1 : 1 + token_count].astype(
        jnp.bfloat16
    )
    returned_part = passed_along(grad_kv_groups[0], "seq", -1)
    grad_local = grad_kv_groups[1:].at[spans_dev - 1].add(returned_part)
    grad_blocks_local = grad_local.astype(jnp.bfloat16).reshape(shards, block_rows, 2, inner_dev)
    returning = lax.all_to_all(
        grad_blocks_local[local_slot], "seq", split_axis=0, concat_axis=0, tiled=True
    )
    grad_kv = returning[destination].reshape(1, owner_rows, 2, inner_dev)
    return (layer_out[None], grad_queries[None], grad_kv, weight_grad)


def solution(mesh):
    in_specs = (
        P("dp", "seq", "tensor"),
        P("dp", "seq", None, "tensor"),
        P("dp", "seq"),
        P("dp", None),
        P("tensor", None, "dp"),
        P("dp", "seq", "tensor"),
    )
    out_specs = (
        P("dp", "seq", "tensor"),
        P("dp", "seq", "tensor"),
        P("dp", "seq", None, "tensor"),
        P("tensor", "seq", "dp"),
    )
    return jax.shard_map(local, mesh=mesh, in_specs=in_specs, out_specs=out_specs, check_vma=False)
```

profile of v0, /device:TPU:17, one launch (start us, length us, event | category | flops | bytes accessed | tf_op | source)
XLA Modules:
  0.0 544.2 jit_solution(1646766976672029594)
XLA Ops:
  11.7 10.0 %all-to-all-start.1 = ((s32[32,1,1]{2,1,0:T(1,128)}), s32[32,1,1]{2,1,0:T(1,128)S(1)}, u32[]{:S(2)}, u32[]{:S(2)}) async-start(s32[32,1,1]{2,1,0:T(1,128)} %copy.132), calls=%async_computation.1 | async-start | bytes 32768 | tf_op jit(solution)/shard_map/all_to_all | solution.py:113
  26.0 3.5 all-to-all-done.1
  29.5 5.0 all-to-all-start
  36.8 47.7 %all-to-all-done = bf16[32,16,2,1024]{3,1,2,0:T(8,128)(2,1)} async-done(((bf16[32,16,2,1024]{3,1,2,0:T(8,128)(2,1)}), bf16[32,16,2,1024]{3,1,2,0:T(8,128)(2,1)}, u32[]{:S(2)}, u32[]{:S(2)}) %all-to-all-start) | async-done | bytes 2097184 | tf_op jit(solution)/shard_map/all_to_all | solution.py:112
  87.1 5.2 collective-permute-start
  94.2 32.1 %collective-permute-done = bf16[256,2,1024]{2,0,1:T(8,128)(2,1)} collective-permute-done((bf16[256,2,1024]{2,0,1:T(8,128)(2,1)S(1)}, bf16[256,2,1024]{2,0,1:T(8,128)(2,1)}, u32[]{:S(2)}, u32[]{:S(2)}) %collective-permute-start) | collective-permute-done | bytes 1048608 | tf_op jit(solution)/shard_map/ppermute | solution.py:17
  132.3 37.2 %all-gather.4.cloned.1.call-done = bf16[8,128,4096]{2,1,0:T(8,128)(2,1)} async-done(((bf16[8,128,2048]{2,1,0:T(8,128)(2,1)}), bf16[8,128,4096]{2,1,0:T(8,128)(2,1)}) %all-gather.4.cloned.1.call-update) | async-done | bytes 8388624 | tf_op jit(solution)/shard_map/all_gather | solution.py:144
  169.5 6.6 %convolution_convert_fusion.1 = bf16[128,1024]{1,0:T(8,128)(2,1)S(1)} fusion(bf16[1024,4096]{1,0:T(8,128)(2,1)} %bitcast.98, bf16[1,128,4096]{2,1,0:T(8,128)(2,1)} %all-gather.6.cloned.1.call-done), kind=kOutput, calls=%fused_computation.28 | convolution fusion | flops 1073872896 | bytes 9699328 | tf_op jit(solution)/shard_map/dot_general | solution.py:150
  179.6 5.2 fusion.11
  189.4 19.5 %copy.151 = f32[8,128,4096]{2,0,1:T(8,128)} copy(f32[8,128,4096]{2,1,0:T(8,128)S(1)} %bitcast.96) | data formatting | bytes 33554432 | tf_op jit(solution)/shard_map/reshape | solution.py:155
  209.0 5.9 %convolution_bitcast_fusion = f32[3,256,1,8,128]{1,4,3,0,2:T(8,128)} fusion(bf16[3,64,8,128]{3,2,1,0:T(8,128)(2,1)} %bitcast.121, bf16[3]{0:T(256)(128)(2,1)} %copy-done.16, f32[3,8,64]{2,1,0:T(8,128)S(1)} %get-tuple-element.50, f32[3,8,64,256]{3,2,1,0:T(8,128)S(1)} %multiply_select_fusion), kind=kOutput, calls=%fused_computation.17 | convolution fusion | flops 102041344 | bytes 5117958 | tf_op jit(solution)/shard_map/ghqk,gqhd->gkhd/dot_general | solution.py:58
  228.6 6.1 %fusion.15 = f32[128,4096]{1,0:T(8,128)} fusion(bf16[1024,4096]{1,0:T(8,128)(2,1)} %bitcast.99, bf16[192,1024]{1,0:T(8,128)(2,1)S(1)} %bitcast.112, bf16[128]{0:T(256)(128)(2,1)S(1)} %copy-done.12), kind=kOutput, calls=%fused_computation.46 | convolution fusion | flops 1073872896 | bytes 10748416 | tf_op jit(solution)/shard_map/dot_general | solution.py:146
  241.5 4.1 copy.149
  245.7 20.3 %collective-permute-done.1 = f32[256,2,1024]{2,0,1:T(8,128)} collective-permute-done((f32[256,2,1024]{2,0,1:T(8,128)}, f32[256,2,1024]{2,0,1:T(8,128)}, u32[]{:S(2)}, u32[]{:S(2)}) %collective-permute-start.1) | collective-permute-done | bytes 2097184 | tf_op jit(solution)/shard_map/ppermute | solution.py:17
  269.0 3.7 gather_fusion.3
  272.6 27.2 %all-to-all-start.2 = ((bf16[32,16,2,1024]{3,1,2,0:T(8,128)(2,1)}), bf16[32,16,2,1024]{3,1,2,0:T(8,128)(2,1)}, u32[]{:S(2)}, u32[]{:S(2)}) async-start(bf16[32,16,2,1024]{3,1,2,0:T(8,128)(2,1)} %gather_fusion.3), calls=%async_computation.3 | async-start | bytes 4194304 | tf_op jit(solution)/shard_map/all_to_all | solution.py:176
  299.9 151.2 %reduce-scatter.8.cloned.1.call-done = f32[8,4,4096]{2,0,1:T(8,128)} async-done(((f32[8,128,4096]{2,0,1:T(8,128)}), f32[8,4,4096]{2,0,1:T(8,128)}) %reduce-scatter.8.cloned.1.call-update) | async-done | bytes 524304 | tf_op jit(solution)/shard_map/reduce_scatter | solution.py:156
  451.2 9.6 %copy.160 = f32[8,4,4096]{1,0,2:T(8,128)} copy(f32[8,4,4096]{2,0,1:T(8,128)} %reduce-scatter.8.cloned.1.call-done) | data formatting | bytes 1048576
  460.8 11.8 %reshape.309 = f32[4096,32]{1,0:T(8,128)} reshape(f32[4096,8,4]{2,1,0:T(8,128)} %bitcast.97) | data formatting | bytes 1048576
  477.0 11.6 %reduce-scatter.6.cloned.1.call-done = f32[128,1024]{1,0:T(8,128)} async-done(((f32[128,4096]{1,0:T(8,128)}), f32[128,1024]{1,0:T(8,128)}) %reduce-scatter.6.cloned.1.call-update) | async-done | bytes 524304 | tf_op jit(solution)/shard_map/reduce_scatter | solution.py:147
  492.8 3.5 copy.153
  496.2 29.7 %reduce-scatter.10.cloned.1.call-done = f32[2048,32]{1,0:T(8,128)} async-done(((f32[4096,32]{1,0:T(8,128)}), f32[2048,32]{1,0:T(8,128)}) %reduce-scatter.10.cloned.1.call-update) | async-done | bytes 262160
  525.9 5.9 %reshape.310 = f32[2048,8,4]{2,1,0:T(8,128)} reshape(f32[2048,32]{1,0:T(8,128)} %reduce-scatter.10.cloned.1.call-done) | data formatting | bytes 524288
  531.8 5.9 %copy.161 = f32[8,4,2048]{2,1,0:T(4,128)} copy(f32[8,4,2048]{1,0,2:T(8,128)} %bitcast.100) | data formatting | bytes 524288
  (106 shorter events, 61.4 us)
Async XLA Ops:
  7.2 125.1 %all-gather.6.cloned.1.call-start = ((), (), s32[]{:S(2)}) async-start(), calls=%async_computation.9 | async-start | bytes 1310720 | tf_op jit(solution)/shard_map/all_gather | solution.py:143
  7.9 161.5 %all-gather.4.cloned.1.call-start = ((), (), s32[]{:S(2)}) async-start(), calls=%async_computation.6 | async-start | bytes 12582912 | tf_op jit(solution)/shard_map/all_gather | solution.py:144
  11.7 17.8 %all-to-all-start.1 = ((s32[32,1,1]{2,1,0:T(1,128)}), s32[32,1,1]{2,1,0:T(1,128)S(1)}, u32[]{:S(2)}, u32[]{:S(2)}) async-start(s32[32,1,1]{2,1,0:T(1,128)} %copy.132), calls=%async_computation.1 | async-start | bytes 32768 | tf_op jit(solution)/shard_map/all_to_all | solution.py:113
  29.5 55.1 %all-to-all-start = ((bf16[32,16,2,1024]{3,1,2,0:T(8,128)(2,1)}), bf16[32,16,2,1024]{3,1,2,0:T(8,128)(2,1)}, u32[]{:S(2)}, u32[]{:S(2)}) async-start(bf16[32,16,2,1024]{3,1,2,0:T(8,128)(2,1)} %gather_fusion), calls=%async_computation | async-start | bytes 4194304 | tf_op jit(solution)/shard_map/all_to_all | solution.py:112
  34.5 416.7 %reduce-scatter.8.cloned.1.call-start = ((), (), s32[]{:S(2)}) async-start(), calls=%async_computation.8 | async-start | bytes 17301504 | tf_op jit(solution)/shard_map/reduce_scatter | solution.py:156
  35.2 1.7 copy-start.13
  86.9 6.8 %copy-start.15 = (s32[1,64]{1,0:T(1,128)S(1)}, s32[1,64]{1,0:T(1,128)}, u32[]{:S(2)}) copy-start(s32[1,64]{1,0:T(1,128)} %param.11) | copy-start | bytes 772
  87.1 39.2 %collective-permute-start = (bf16[256,2,1024]{2,0,1:T(8,128)(2,1)S(1)}, bf16[256,2,1024]{2,0,1:T(8,128)(2,1)}, u32[]{:S(2)}, u32[]{:S(2)}) collective-permute-start(bf16[256,2,1024]{2,0,1:T(8,128)(2,1)S(1)} %bitcast.119), channel_id=1, source_target_pairs={{0,8},{8,16},{16,24},{24,32},{32,40},{40,48},{48,56},{56,64},{64,7... | collective-permute-start | bytes 3145736 | tf_op jit(solution)/shard_map/ppermute | solution.py:17
  130.6 46.8 %copy-start.1 = (bf16[3,256,1,1024]{1,3,0,2:T(8,128)(2,1)}, bf16[3,256,1,1024]{1,3,0,2:T(8,128)(2,1)S(1)}, u32[]{:S(2)}) copy-start(bf16[3,256,1,1024]{1,3,0,2:T(8,128)(2,1)S(1)} %copy.137) | copy-start | bytes 4718596
  169.5 6.7 %copy-start.11 = (bf16[1,128,1024]{2,1,0:T(8,128)(2,1)S(1)}, bf16[1,128,1024]{2,1,0:T(8,128)(2,1)}, u32[]{:S(2)}) copy-start(bf16[1,128,1024]{2,1,0:T(8,128)(2,1)} %param.8) | copy-start | bytes 786436
  177.8 1.8 copy-start.10
  184.8 1.4 copy-start.7
  186.3 3.2 copy-start.8
  209.0 279.5 %reduce-scatter.6.cloned.1.call-start = ((), (), s32[]{:S(2)}) async-start(), calls=%async_computation.7 | async-start | bytes 2621440 | tf_op jit(solution)/shard_map/reduce_scatter | solution.py:147
  217.1 1.2 copy-start.5
  218.3 1.9 copy-start.3
  222.5 6.1 %copy-start.9 = (bf16[24,8,8,128]{3,1,2,0:T(8,128)(2,1)S(1)}, bf16[24,8,8,128]{3,1,2,0:T(8,128)(2,1)}, u32[]{:S(2)}) copy-start(bf16[24,8,8,128]{3,1,2,0:T(8,128)(2,1)} %copy-done.8) | copy-start | bytes 1179652
  222.5 6.1 %copy-start.12 = (bf16[128]{0:T(256)(128)(2,1)S(1)}, bf16[128]{0:T(256)(128)(2,1)}, u32[]{:S(2)}) copy-start(bf16[128]{0:T(256)(128)(2,1)} %slice.81) | copy-start | bytes 772
  225.6 40.3 %collective-permute-start.1 = (f32[256,2,1024]{2,0,1:T(8,128)}, f32[256,2,1024]{2,0,1:T(8,128)}, u32[]{:S(2)}, u32[]{:S(2)}) collective-permute-start(f32[256,2,1024]{2,0,1:T(8,128)} %copy.147), channel_id=1, source_target_pairs={{8,0},{16,8},{24,16},{32,24},{40,32},{48,40},{56,48},{64,56},{72,6... | collective-permute-start | bytes 6291464 | tf_op jit(solution)/shard_map/ppermute | solution.py:17
  241.5 24.4 %copy-start.4 = (f32[256,2,1024]{2,0,1:T(8,128)S(1)}, f32[256,2,1024]{2,0,1:T(8,128)}, u32[]{:S(2)}) copy-start(f32[256,2,1024]{2,0,1:T(8,128)} %copy.148) | copy-start | bytes 6291460
  272.6 217.7 %all-to-all-start.2 = ((bf16[32,16,2,1024]{3,1,2,0:T(8,128)(2,1)}), bf16[32,16,2,1024]{3,1,2,0:T(8,128)(2,1)}, u32[]{:S(2)}, u32[]{:S(2)}) async-start(bf16[32,16,2,1024]{3,1,2,0:T(8,128)(2,1)} %gather_fusion.3), calls=%async_computation.3 | async-start | bytes 4194304 | tf_op jit(solution)/shard_map/all_to_all | solution.py:176
  299.9 226.0 %reduce-scatter.10.cloned.1.call-start = ((), (), s32[]{:S(2)}) async-start(), calls=%async_computation.10 | async-start | bytes 3145728
  460.8 11.9 %copy-start.6 = (f32[3,8,64,256]{3,2,1,0:T(8,128)S(1)}, f32[3,8,64,256]{3,2,1,0:T(8,128)}, u32[]{:S(2)}) copy-start(f32[3,8,64,256]{3,2,1,0:T(8,128)} %copy-done.5) | copy-start | bytes 4718596
  472.6 1.4 copy-start.2
  (3 other events, 1.8 us)
Sparse Core Ops, SparseCore 0:
  9.8 28.3 all-gather.5
  40.0 129.3 all-gather.3
  209.1 241.9 reduce-scatter.7
  454.1 34.3 reduce-scatter.5
  491.0 34.8 reduce-scatter.9
where the time goes:
time: 550 us; the launch traced here: 544 us
  waiting for transfers between devices  335 us (61%)
  local copies, waits for them, and re-layouts  92.8 us (17%)
  starting transfers between devices  50.6 us (9%)
  matrix products  32.8 us (6%)
  other arithmetic  19.1 us (3%)
  between operations  14.2 us (3%)
    reduce_scatter x1, waiting for transfers between devices, local(): lax.psum_scatter(weight_terms, 'seq', scatter_dimension=1, tiled=True)  151 us
    ppermute x2, waiting for transfers between devices, passed_along(): lax.ppermute(value, axis, [(source, source + steps) for source in range(i...  52.4 us
    all_to_all x1, waiting for transfers between devices, local(): lax.all_to_all(outgoing, 'seq', split_axis=0, concat_axis=0, tiled=True)  47.7 us
    unnamed x43, local copies, waits for them, and re-layouts  42.1 us
    all_gather x1, waiting for transfers between devices, local(): full_weight = lax.all_gather(out_weight, 'dp', axis=2, tiled=True)  37.2 us
    unnamed x6, waiting for transfers between devices  31.1 us
    all_to_all x1, starting transfers between devices, local(): lax.all_to_all(grad_blocks_local[local_slot], 'seq', split_axis=0, concat...  27.2 us
    reshape x1, local copies, waits for them, and re-layouts, local(): weight_terms = lax.dot_general(context, grad_full, (((0,), (0,)), ((), ()...  19.5 us
  transfers between devices with their start and end apart: 10, of which 8 were waited for; matrix products, arithmetic and copies ran while one was open for 16% of the time, Pallas kernels for 0%

commit v1 on v0

v1 whole, which is shorter than its diff:
```python
import functools

import jax
import jax.numpy as jnp
from jax import lax
from jax.experimental import pallas as pl
from jax.experimental.pallas import tpu as pltpu
from jax.sharding import PartitionSpec as P

CLEN = 64
NLEN = 128
HD = 128
BLK = 16
SHARDS = 32
TENSOR = 4
REPLICAS = 2
NEG_FILL = -1e30
CHUNKS = 2
AXES = ("seq", "tensor", "dp")


def moved(value, where):
    pairs = []
    for s in range(SHARDS):
        for t in range(TENSOR):
            for d in range(REPLICAS):
                to = where(s, t, d)
                if to is not None:
                    pairs.append(((s * TENSOR + t) * REPLICAS + d, (to[0] * TENSOR + to[1]) * REPLICAS + to[2]))
    return lax.ppermute(value, AXES, pairs)


def to_previous(value):
    return moved(value, lambda s, t, d: (s - 1, t, d) if s > 0 else None)


def to_next(value):
    return moved(value, lambda s, t, d: (s + 1, t, d) if s + 1 < SHARDS else None)


def flip_seq(value, bits):
    return moved(value, lambda s, t, d: (s ^ bits, t, d))


def flip_dp(value):
    return moved(value, lambda s, t, d: (s, t, 1 - d))


def pick(index, options):
    chosen = options[-1]
    for at in range(len(options) - 2, -1, -1):
        chosen = jnp.where(index == at, options[at], chosen)
    return chosen


def to_windows(rows):
    half = rows.shape[0] // 2
    after = to_previous(rows[:half])
    own = lax.broadcasted_iota(jnp.int32, (half, 1), 0) == half - 1
    return jnp.concatenate([rows[half:], jnp.where(own, rows[:half], after)], axis=0)


def from_windows(rows):
    half = rows.shape[0] // 2
    before = to_next(rows[half:])
    own = lax.broadcasted_iota(jnp.int32, (half, 1), 0) == half - 1
    return jnp.concatenate([jnp.where(own, rows[half:], before), rows[:half]], axis=0)


def attend_kernel(bias_ref, query_ref, grad_ref, kv_ref, grad_kv_ref, context_ref, grad_query_ref):
    rows, size = query_ref.shape
    blocks = kv_ref.shape[0]
    keys = blocks * BLK
    scale = size ** (-0.5)
    query = query_ref[...]
    grad = grad_ref[...]
    key = kv_ref[:, :BLK, :].reshape(keys, size)
    value = kv_ref[:, BLK:, :].reshape(keys, size)
    row = lax.broadcasted_iota(jnp.int32, (rows, 1), 0)
    second = (row >= CLEN - 1) & (row < rows - 1)
    bias = jnp.where(second, bias_ref[1:2, :], bias_ref[0:1, :])
    nt = (((1,), (1,)), ((), ()))
    tn = (((0,), (0,)), ((), ()))
    scores = lax.dot_general(query, key, nt, preferred_element_type=jnp.float32) * scale + bias
    raw = jnp.exp(scores - jnp.max(scores, axis=-1, keepdims=True))
    soft = raw * (1.0 / jnp.sum(raw, axis=-1, keepdims=True))
    low = soft.astype(jnp.bfloat16)
    context = jnp.dot(low, value, preferred_element_type=jnp.float32).astype(jnp.bfloat16)
    context_ref[...] = context
    grad_weights = lax.dot_general(grad, value, nt, preferred_element_type=jnp.float32)
    delta = jnp.sum(grad.astype(jnp.float32) * context.astype(jnp.float32), axis=-1, keepdims=True)
    grad_scores = (soft * (grad_weights - delta) * scale).astype(jnp.bfloat16)
    grad_query_ref[...] = jnp.dot(grad_scores, key, preferred_element_type=jnp.float32).astype(jnp.bfloat16)
    grad_key = lax.dot_general(grad_scores, query, tn, preferred_element_type=jnp.float32)
    grad_value = lax.dot_general(low, grad, tn, preferred_element_type=jnp.float32)
    grad_kv_ref[:, :BLK, :] = grad_key.astype(jnp.bfloat16).reshape(blocks, BLK, size)
    grad_kv_ref[:, BLK:, :] = grad_value.astype(jnp.bfloat16).reshape(blocks, BLK, size)


def attend(bias, query, grad, kv, first_head):
    rows = query.shape[0]
    blocks, block_rows, width = kv.shape
    heads = width // HD
    per_head = pl.BlockSpec((rows, HD), lambda h: (0, h))
    shifted = pl.BlockSpec((rows, HD), lambda h: (0, h + first_head))
    block_spec = pl.BlockSpec((blocks, block_rows, HD), lambda h: (0, 0, h))
    keys = blocks * BLK
    return pl.pallas_call(
        attend_kernel,
        grid=(heads,),
        in_specs=[pl.BlockSpec((2, keys), lambda h: (0, 0)), shifted, shifted, block_spec],
        out_specs=[block_spec, per_head, per_head],
        out_shape=[
            jax.ShapeDtypeStruct(kv.shape, jnp.bfloat16),
            jax.ShapeDtypeStruct((rows, width), jnp.bfloat16),
            jax.ShapeDtypeStruct((rows, width), jnp.bfloat16),
        ],
        compiler_params=pltpu.CompilerParams(vmem_limit_bytes=32 * 1024 * 1024),
        cost_estimate=pl.CostEstimate(
            flops=heads * 12 * rows * keys * HD,
            bytes_accessed=4 * kv.size + 8 * rows * width,
            transcendentals=heads * rows * keys,
        ),
    )(bias, query, grad, kv)


def summed_over_z(parts, seq_place):
    z = seq_place // 4
    kept = parts
    for bit in range(3):
        mine = (z >> bit) & 1
        pairs = kept.reshape((kept.shape[0] // 2, 2) + kept.shape[1:])
        keep = jnp.where(mine == 0, pairs[:, 0], pairs[:, 1])
        send = jnp.where(mine == 0, pairs[:, 1], pairs[:, 0]).astype(jnp.bfloat16)
        kept = keep + flip_seq(send, 4 << bit).astype(jnp.float32)
    return kept[0]


def local(queries, neighbour_kv, block_target, neighbour_count, out_weight, grad_mixed):
    seq_place = lax.axis_index("seq")
    tensor_place = lax.axis_index("tensor")
    dp_place = lax.axis_index("dp")
    core = seq_place % 2
    pair = (seq_place // 2) % 2
    rows, inner_dev = queries.shape[1:]
    heads_dev = inner_dev // HD
    chunk_width = inner_dev // CHUNKS

    target = block_target[0]
    destination = target // SHARDS
    matches = destination[None, :] == jnp.arange(SHARDS)[:, None]
    send_order = jnp.sum(jnp.where(matches, jnp.arange(SHARDS)[None, :], 0), axis=1)
    blocks = neighbour_kv[0].reshape(SHARDS, BLK, 2, inner_dev).transpose(0, 2, 1, 3)
    outgoing = blocks.reshape(SHARDS, 2 * BLK, inner_dev)[send_order]
    incoming = [
        lax.all_to_all(
            outgoing[:, :, at * chunk_width : (at + 1) * chunk_width], "seq", split_axis=0, concat_axis=0, tiled=True
        )
        for at in range(CHUNKS)
    ]
    targets_all = lax.all_gather(target, "seq", axis=0, tiled=False)
    mine = targets_all // SHARDS == seq_place
    slot = jnp.sum(jnp.where(mine, targets_all % SHARDS, 0), axis=1)
    counts = lax.dynamic_slice(neighbour_count[0], (2 * seq_place,), (2,))
    live = (slot[None, :] // 16 == jnp.arange(2)[:, None]) & (slot[None, :] % 16 // 8 < counts[:, None])
    bias = jnp.where(jnp.repeat(live, BLK, axis=1), 0.0, NEG_FILL).astype(jnp.float32)

    query_rows = to_windows(queries[0])
    grad_rows = to_windows(grad_mixed[0])
    rounds = [
        moved(grad_rows, lambda s, t, d, j=j: (s, (2 * d + t % 2) ^ j, t // 2)) for j in range(4)
    ]
    quarter = [pick(tensor_place ^ at, rounds) for at in range(4)]
    weight = out_weight.reshape(inner_dev, -1)
    grad_half = jnp.concatenate(
        [jnp.concatenate(quarter[:2], axis=1), jnp.concatenate(quarter[2:], axis=1)], axis=0
    )
    partial_grad = lax.dot_general(
        grad_half, weight, (((1,), (1,)), ((), ())), preferred_element_type=jnp.float32
    ).reshape(2, rows, inner_dev)
    grad_own = jnp.where(dp_place == 0, partial_grad[0], partial_grad[1])
    grad_other = jnp.where(dp_place == 0, partial_grad[1], partial_grad[0]).astype(jnp.bfloat16)
    grad_context = (grad_own + flip_dp(grad_other).astype(jnp.float32)).astype(jnp.bfloat16)

    columns = [grad_half[:, : grad_half.shape[1] // 2], grad_half[:, grad_half.shape[1] // 2 :]]
    columns_own = jnp.where(core == 0, columns[0], columns[1])
    columns_other = jnp.where(core == 0, columns[1], columns[0])
    grad_group = jnp.concatenate(
        [columns_own, flip_seq(columns_other, 1), flip_seq(columns_own, 2), flip_seq(columns_other, 3)], axis=0
    )

    grad_blocks, contexts, grad_query_parts, weight_parts = [], [], [], []
    for at in range(CHUNKS):
        sent_back, context, grad_query = attend(bias, query_rows, grad_context, incoming[at], at * heads_dev // CHUNKS)
        grad_blocks.append(lax.all_to_all(sent_back, "seq", split_axis=0, concat_axis=0, tiled=True))
        grad_query_parts.append(grad_query)
        context_other = flip_dp(context)
        both = jnp.concatenate(
            [jnp.where(dp_place == 0, context, context_other), jnp.where(dp_place == 0, context_other, context)], axis=0
        )
        contexts.append(both)
        half = chunk_width // 2
        half_own = jnp.where(pair == 0, both[:, :half], both[:, half:])
        half_other = jnp.where(pair == 0, both[:, half:], both[:, :half])
        context_group = jnp.concatenate(
            [half_own, flip_seq(half_own, 1), flip_seq(half_other, 2), flip_seq(half_other, 3)], axis=0
        )
        terms = lax.dot_general(
            context_group, grad_group, (((0,), (0,)), ((), ())), preferred_element_type=jnp.float32
        )
        terms = terms.reshape(half // HD, 8, HD // 8, -1).transpose(1, 0, 2, 3)
        weight_parts.append(summed_over_z(terms, seq_place))

    weight_sum = jnp.stack(weight_parts, axis=0)
    weight_sum = weight_sum.reshape(weight_sum.shape[:2] + (4, 4, weight_sum.shape[-1]))
    place = 2 * pair + core
    received = [
        pick(place, [weight_sum[:, :, at] for at in range(4)])
    ] + [
        flip_seq(pick(place ^ bits, [weight_sum[:, :, at] for at in range(4)]), bits) for bits in (1, 2, 3)
    ]
    by_pair = []
    for p in range(2):
        by_core = [pick((2 * p + c) ^ place, received) for c in range(2)]
        by_pair.append(jnp.concatenate(by_core, axis=-1))
    weight_grad = jnp.stack(by_pair, axis=1).reshape(heads_dev, 4, -1)

    context_both = jnp.concatenate(contexts, axis=1)
    partial_out = jnp.dot(context_both, weight, preferred_element_type=jnp.float32).astype(jnp.bfloat16)
    width = partial_out.shape[1] // 2
    total = None
    for j in range(4):
        piece = tensor_place ^ j
        sent = lax.dynamic_slice(partial_out, (piece // 2 * rows, piece % 2 * width), (rows, width))
        came = moved(sent, lambda s, t, d, j=j: (s, 2 * d + (t ^ j) % 2, (t ^ j) // 2)).astype(jnp.float32)
        total = came if total is None else total + came
    layer_out = from_windows(total.astype(jnp.bfloat16))
    grad_queries = from_windows(jnp.concatenate(grad_query_parts, axis=1))

    returned = jnp.concatenate(grad_blocks, axis=2)[destination]
    grad_kv = returned.reshape(SHARDS, 2, BLK, inner_dev).transpose(0, 2, 1, 3)
    return (
        layer_out[None],
        grad_queries[None],
        grad_kv.reshape(1, SHARDS * BLK, 2, inner_dev),
        weight_grad,
    )


def solution(mesh):
    in_specs = (
        P("dp", "seq", "tensor"),
        P("dp", "seq", None, "tensor"),
        P("dp", "seq"),
        P("dp", None),
        P("tensor", None, "dp"),
        P("dp", "seq", "tensor"),
    )
    out_specs = (
        P("dp", "seq", "tensor"),
        P("dp", "seq", "tensor"),
        P("dp", "seq", None, "tensor"),
        P("tensor", "seq", "dp"),
    )
    return jax.shard_map(local, mesh=mesh, in_specs=in_specs, out_specs=out_specs, check_vma=False)
```

time: 550 us -> 265 us (0.48)
  the two profiles are of different devices: /device:TPU:17 before, /device:TPU:11 now
where the time goes in v1:
time: 265 us; the launch traced here: 264 us
  starting transfers between devices  117 us (44%)
  waiting for transfers between devices  54.2 us (20%)
  blocking collectives  45.6 us (17%)
  local copies, waits for them, and re-layouts  18.2 us (7%)
  matrix products  11.5 us (4%)
  Pallas kernels  8.85 us (3%)
  other arithmetic  7.39 us (3%)
    ppermute x33, starting transfers between devices, moved(): return lax.ppermute(value, AXES, pairs)  73.4 us
    all_gather x1, blocking collectives, local(): targets_all = lax.all_gather(target, 'seq', axis=0, tiled=False)  45.6 us
    ppermute x33, waiting for transfers between devices, moved(): return lax.ppermute(value, AXES, pairs)  34.2 us
    all_to_all x2, starting transfers between devices, local(): lax.all_to_all(outgoing[:, :, at * chunk_width:(at + 1) * chunk_width], '...  23.1 us
    all_to_all x2, starting transfers between devices, local(): lax.all_to_all(sent_back, 'seq', split_axis=0, concat_axis=0, tiled=True)  20.3 us
    all_to_all x2, waiting for transfers between devices, local(): lax.all_to_all(sent_back, 'seq', split_axis=0, concat_axis=0, tiled=True)  18.2 us
    pallas_call x2, Pallas kernels, attend(): pl.pallas_call(attend_kernel, grid=(heads,), in_specs=[pl.BlockSpec((2, k...  8.85 us
  transfers between devices with their start and end apart: 37, of which 12 were waited for; matrix products, arithmetic and copies ran while one was open for 7% of the time, Pallas kernels for 3%

profile of v1, /device:TPU:11, one launch (start us, length us, event | category | flops | bytes accessed | tf_op | source)
XLA Modules:
  0.0 264.0 jit_solution(4940656737952029800)
XLA Ops:
  8.8 10.5 %all-to-all-start.1 = ((bf16[32,32,512]{2,1,0:T(8,128)(2,1)}), bf16[32,32,512]{2,1,0:T(8,128)(2,1)S(1)}, u32[]{:S(2)}, u32[]{:S(2)}) async-start(bf16[32,32,512]{2,1,0:T(8,128)(2,1)} %get-tuple-element.19), calls=%async_computation.1 | async-start | bytes 2097152 | tf_op jit(solution)/shard_map/all_to_all | solution.py:156
  23.7 45.6 %all-gather = s32[32,1,32]{2,1,0:T(1,128)S(1)} all-gather(s32[1,1,32]{2,1,0:T(1,128)S(1)} %bitcast.238), channel_id=1, replica_groups=mesh['seq'=32,'tensor'=4,'dp'=2] {'seq'}, dimensions={0}, use_global_device_ids=true | all-gather | bytes 4224 | tf_op jit(solution)/shard_map/all_gather | solution.py:161
  72.4 7.3 %collective-permute-start.4 = (bf16[128,1024]{1,0:T(8,128)(2,1)}, bf16[128,1024]{1,0:T(8,128)(2,1)S(1)}, u32[]{:S(2)}, u32[]{:S(2)}) collective-permute-start(bf16[128,1024]{1,0:T(8,128)(2,1)} %pad_maximum_fusion.5), channel_id=1, source_target_pairs={{0,4},{1,0},{2,6},{3,2},{4,5},{5,1},{6,7},{7,3},{8,12},{9,8},{10,1... | collective-permute-start | bytes 786440 | tf_op jit(solution)/shard_map/ppermute | solution.py:30
  79.7 12.6 %all-to-all-start = ((bf16[32,32,512]{2,1,0:T(8,128)(2,1)}), bf16[32,32,512]{2,1,0:T(8,128)(2,1)S(1)}, u32[]{:S(2)}, u32[]{:S(2)}) async-start(bf16[32,32,512]{2,1,0:T(8,128)(2,1)} %get-tuple-element.18), calls=%async_computation | async-start | bytes 2097152 | tf_op jit(solution)/shard_map/all_to_all | solution.py:156
  93.9 3.5 %fusion.56 = f32[256,1024]{1,0:T(8,128)S(1)} fusion(bf16[1024,2048]{1,0:T(8,128)(2,1)} %bitcast.239, bf16[128,1024]{1,0:T(8,128)(2,1)S(1)} %get-tuple-element.29, bf16[128,1024]{1,0:T(8,128)(2,1)S(1)} %get-tuple-element.30, bf16[128,1024]{1,0:T(8,128)(2,1)S(1)} %get-tuple-element.31, bf16[128,1024]{1,0:T(8,128)(2,1)S(1)} %get-tuple-element.28), kind=kOutput, calls=%fused_computation.159 | convolution fusion | flops 1077936128 | bytes 6291456 | tf_op jit(solution)/shard_map/dot_general | solution.py:178
  101.3 3.9 %collective-permute-start.20 = (bf16[256,1024]{1,0:T(8,128)(2,1)}, bf16[256,1024]{1,0:T(8,128)(2,1)}, u32[]{:S(2)}, u32[]{:S(2)}) collective-permute-start(bf16[256,1024]{1,0:T(8,128)(2,1)} %get-tuple-element.23), channel_id=1, source_target_pairs={{0,24},{1,25},{2,26},{3,27},{4,28},{5,29},{6,30},{7,31},{8,16},{9,... | collective-permute-start | bytes 1572872 | tf_op jit(solution)/shard_map/ppermute | solution.py:30
  105.3 6.1 %collective-permute-done.6 = bf16[128,1024]{1,0:T(8,128)(2,1)S(1)} collective-permute-done((bf16[128,1024]{1,0:T(8,128)(2,1)S(1)}, bf16[128,1024]{1,0:T(8,128)(2,1)S(1)}, u32[]{:S(2)}, u32[]{:S(2)}) %collective-permute-start.6) | collective-permute-done | bytes 262176 | tf_op jit(solution)/shard_map/ppermute | solution.py:30
  111.5 4.5 %shard_map.94 = (bf16[32,32,512]{2,1,0:T(8,128)(2,1)}, bf16[128,512]{1,0:T(8,128)(2,1)S(1)}, bf16[128,512]{1,0:T(8,128)(2,1)S(1)}) custom-call(f32[2,512]{1,0:T(2,128)S(1)} %select_n.605.bias_ref, bf16[128,1024]{1,0:T(8,128)(2,1)S(1)} %pad_maximum_fusion.4.query_ref, bf16[128,1024]{1,0:T(8,128)(2,1)S(1)} %add_convert_fusion.1.grad_ref, ...), custom_call_target="tpu_custom_call" | custom-call | flops 402653184 | bytes 2621440 | tf_op jit(solution)/shard_map/pallas_call | solution.py:108
  120.5 4.4 %shard_map.93 = (bf16[32,32,512]{2,1,0:T(8,128)(2,1)}, bf16[128,512]{1,0:T(8,128)(2,1)S(1)}, bf16[128,512]{1,0:T(8,128)(2,1)S(1)}) custom-call(f32[2,512]{1,0:T(2,128)S(1)} %select_n.605.bias_ref, bf16[128,1024]{1,0:T(8,128)(2,1)S(1)} %pad_maximum_fusion.4.query_ref, bf16[128,1024]{1,0:T(8,128)(2,1)S(1)} %add_convert_fusion.1.grad_ref, ...), custom_call_target="tpu_custom_call" | custom-call | flops 402653184 | bytes 2621440 | tf_op jit(solution)/shard_map/pallas_call | solution.py:108
  128.3 8.5 %all-to-all-start.3 = ((bf16[32,32,512]{2,1,0:T(8,128)(2,1)}), bf16[32,32,512]{2,1,0:T(8,128)(2,1)S(1)}, u32[]{:S(2)}, u32[]{:S(2)}) async-start(bf16[32,32,512]{2,1,0:T(8,128)(2,1)} %get-tuple-element.15), calls=%async_computation.3 | async-start | bytes 2097152 | tf_op jit(solution)/shard_map/all_to_all | solution.py:195
  136.8 4.2 %collective-permute-done.8 = bf16[128,512]{1,0:T(8,128)(2,1)S(1)} collective-permute-done((bf16[128,512]{1,0:T(8,128)(2,1)S(1)}, bf16[128,512]{1,0:T(8,128)(2,1)S(1)}, u32[]{:S(2)}, u32[]{:S(2)}) %collective-permute-start.8) | collective-permute-done | bytes 131104 | tf_op jit(solution)/shard_map/ppermute | solution.py:30
  144.9 3.5 %convolution_convert_fusion = bf16[256,2048]{1,0:T(8,128)(2,1)S(1)} fusion(bf16[1024,2048]{1,0:T(8,128)(2,1)} %bitcast.240, bf16[128,512]{1,0:T(8,128)(2,1)S(1)} %get-tuple-element.48, bf16[128,512]{1,0:T(8,128)(2,1)S(1)} %get-tuple-element.47, bf16[128,512]{1,0:T(8,128)(2,1)S(1)} %get-tuple-element.46, bf16[128,512]{1,0:T(8,128)(2,1)S(1)} %get-tuple-element.45), kind=kOutput, calls=%fused_computation.2 | convolution fusion | flops 1076363264 | bytes 5767168 | tf_op jit(solution)/shard_map/dot_general | solution.py:229
  148.4 3.7 %collective-permute-start.24 = (bf16[256,256]{1,0:T(8,128)(2,1)S(1)}, bf16[256,256]{1,0:T(8,128)(2,1)S(1)}, u32[]{:S(2)}, u32[]{:S(2)}) collective-permute-start(bf16[256,256]{1,0:T(8,128)(2,1)S(1)} %get-tuple-element.39), channel_id=1, source_target_pairs={{0,8},{1,9},{2,10},{3,11},{4,12},{5,13},{6,14},{7,15},{8,0},{9,1},... | collective-permute-start | bytes 393224 | tf_op jit(solution)/shard_map/ppermute | solution.py:30
  157.2 9.9 %collective-permute-start.15 = (bf16[256,256]{1,0:T(8,128)(2,1)S(1)}, bf16[256,256]{1,0:T(8,128)(2,1)S(1)}, u32[]{:S(2)}, u32[]{:S(2)}) collective-permute-start(bf16[256,256]{1,0:T(8,128)(2,1)S(1)} %get-tuple-element.37), channel_id=1, source_target_pairs={{0,8},{1,9},{2,10},{3,11},{4,12},{5,13},{6,14},{7,15},{8,0},{9,1},... | collective-permute-start | bytes 393224 | tf_op jit(solution)/shard_map/ppermute | solution.py:30
  175.2 4.4 %collective-permute-start.14 = (bf16[64,1024]{1,0:T(8,128)(2,1)S(1)}, bf16[64,1024]{1,0:T(8,128)(2,1)S(1)}, u32[]{:S(2)}, u32[]{:S(2)}) collective-permute-start(bf16[64,1024]{1,0:T(8,128)(2,1)S(1)} %copy-done.3), channel_id=1, source_target_pairs={{0,8},{1,9},{2,10},{3,11},{4,12},{5,13},{6,14},{7,15},{8,16},{9,17... | collective-permute-start | bytes 393224 | tf_op jit(solution)/shard_map/ppermute | solution.py:30
  179.6 6.9 %collective-permute-done.11 = bf16[128,1024]{1,0:T(8,128)(2,1)S(1)} collective-permute-done((bf16[128,1024]{1,0:T(8,128)(2,1)S(1)}, bf16[128,1024]{1,0:T(8,128)(2,1)S(1)}, u32[]{:S(2)}, u32[]{:S(2)}) %collective-permute-start.11) | collective-permute-done | bytes 262176 | tf_op jit(solution)/shard_map/ppermute | solution.py:30
  189.1 3.2 %collective-permute-start.13 = (bf16[64,1024]{1,0:T(8,128)(2,1)S(1)}, bf16[64,1024]{1,0:T(8,128)(2,1)S(1)}, u32[]{:S(2)}, u32[]{:S(2)}) collective-permute-start(bf16[64,1024]{1,0:T(8,128)(2,1)S(1)} %slice.196), channel_id=1, source_target_pairs={{0,8},{1,9},{2,10},{3,11},{4,12},{5,13},{6,14},{7,15},{8,16},{9,17... | collective-permute-start | bytes 393224 | tf_op jit(solution)/shard_map/ppermute | solution.py:30
  192.5 4.8 %collective-permute-start.28 = (bf16[2,2,16,1024]{3,2,1,0:T(8,128)(2,1)S(1)}, bf16[2,2,16,1024]{3,2,1,0:T(8,128)(2,1)S(1)}, u32[]{:S(2)}, u32[]{:S(2)}) collective-permute-start(bf16[2,2,16,1024]{3,2,1,0:T(8,128)(2,1)S(1)} %fusion.31), channel_id=1, source_target_pairs={{0,64},{1,65},{2,66},{3,67},{4,68},{5,69},{6,70},{7,71},{8,72},{9,... | collective-permute-start | bytes 393224 | tf_op jit(solution)/shard_map/ppermute | solution.py:30
  199.0 7.5 %collective-permute-done.28 = bf16[2,2,16,1024]{3,2,1,0:T(8,128)(2,1)S(1)} collective-permute-done((bf16[2,2,16,1024]{3,2,1,0:T(8,128)(2,1)S(1)}, bf16[2,2,16,1024]{3,2,1,0:T(8,128)(2,1)S(1)}, u32[]{:S(2)}, u32[]{:S(2)}) %collective-permute-start.28) | collective-permute-done | bytes 131104 | tf_op jit(solution)/shard_map/ppermute | solution.py:30
  209.4 5.2 %collective-permute-start.23 = (bf16[1,2,16,1024]{3,2,1,0:T(8,128)(2,1)S(1)}, bf16[1,2,16,1024]{3,2,1,0:T(8,128)(2,1)S(1)}, u32[]{:S(2)}, u32[]{:S(2)}) collective-permute-start(bf16[1,2,16,1024]{3,2,1,0:T(8,128)(2,1)S(1)} %fusion.34), channel_id=1, source_target_pairs={{0,128},{1,129},{2,130},{3,131},{4,132},{5,133},{6,134},{7,135},{8... | collective-permute-start | bytes 196616 | tf_op jit(solution)/shard_map/ppermute | solution.py:30
  214.6 11.8 %all-to-all-start.2 = ((bf16[32,32,512]{2,1,0:T(8,128)(2,1)}), bf16[32,32,512]{2,1,0:T(8,128)(2,1)}, u32[]{:S(2)}, u32[]{:S(2)}) async-start(bf16[32,32,512]{2,1,0:T(8,128)(2,1)} %get-tuple-element.14), calls=%async_computation.2 | async-start | bytes 2097152 | tf_op jit(solution)/shard_map/all_to_all | solution.py:195
  231.2 4.7 %collective-permute-done.32 = f32[2,2,4,1024]{3,1,2,0:T(2,128)S(1)} collective-permute-done((f32[2,2,4,1024]{3,1,2,0:T(2,128)S(1)}, f32[2,2,4,1024]{3,1,2,0:T(2,128)S(1)}, u32[]{:S(2)}, u32[]{:S(2)}) %collective-permute-start.32) | collective-permute-done | bytes 65568 | tf_op jit(solution)/shard_map/ppermute | solution.py:30
  237.2 18.2 %all-to-all-done.2 = bf16[32,32,512]{2,1,0:T(8,128)(2,1)} async-done(((bf16[32,32,512]{2,1,0:T(8,128)(2,1)}), bf16[32,32,512]{2,1,0:T(8,128)(2,1)}, u32[]{:S(2)}, u32[]{:S(2)}) %all-to-all-start.2) | async-done | bytes 1048608 | tf_op jit(solution)/shard_map/all_to_all | solution.py:195
  258.9 5.1 %copy.95 = bf16[32,16,2,1024]{3,2,1,0:T(2,128)(2,1)} copy(bf16[32,16,2,1024]{3,1,2,0:T(8,128)(2,1)} %bitcast.213) | data formatting | bytes 4194304 | tf_op jit(solution)/shard_map/transpose | solution.py:241
  (132 shorter events, 62.8 us)
Async XLA Ops:
  8.8 70.9 %all-to-all-start.1 = ((bf16[32,32,512]{2,1,0:T(8,128)(2,1)}), bf16[32,32,512]{2,1,0:T(8,128)(2,1)S(1)}, u32[]{:S(2)}, u32[]{:S(2)}) async-start(bf16[32,32,512]{2,1,0:T(8,128)(2,1)} %get-tuple-element.19), calls=%async_computation.1 | async-start | bytes 2097152 | tf_op jit(solution)/shard_map/all_to_all | solution.py:156
  19.4 50.3 %collective-permute-start.1 = (bf16[64,1024]{1,0:T(8,128)(2,1)S(1)}, bf16[64,1024]{1,0:T(8,128)(2,1)S(1)}, u32[]{:S(2)}, u32[]{:S(2)}) collective-permute-start(bf16[64,1024]{1,0:T(8,128)(2,1)S(1)} %get-tuple-element.50), channel_id=1, source_target_pairs={{8,0},{9,1},{10,2},{11,3},{12,4},{13,5},{14,6},{15,7},{16,8},{17,9... | collective-permute-start | bytes 393224 | tf_op jit(solution)/shard_map/ppermute | solution.py:30
  21.7 48.0 %collective-permute-start = (bf16[64,1024]{1,0:T(8,128)(2,1)S(1)}, bf16[64,1024]{1,0:T(8,128)(2,1)S(1)}, u32[]{:S(2)}, u32[]{:S(2)}) collective-permute-start(bf16[64,1024]{1,0:T(8,128)(2,1)S(1)} %get-tuple-element.52), channel_id=1, source_target_pairs={{8,0},{9,1},{10,2},{11,3},{12,4},{13,5},{14,6},{15,7},{16,8},{17,9... | collective-permute-start | bytes 393224 | tf_op jit(solution)/shard_map/ppermute | solution.py:30
  70.5 22.3 %collective-permute-start.2 = (bf16[128,1024]{1,0:T(8,128)(2,1)}, bf16[128,1024]{1,0:T(8,128)(2,1)S(1)}, u32[]{:S(2)}, u32[]{:S(2)}) collective-permute-start(bf16[128,1024]{1,0:T(8,128)(2,1)} %pad_maximum_fusion.5), channel_id=1, source_target_pairs={{0,0},{1,4},{2,2},{3,6},{4,1},{5,5},{6,3},{7,7},{8,8},{9,12},{10,1... | collective-permute-start | bytes 786440 | tf_op jit(solution)/shard_map/ppermute | solution.py:30
  72.1 20.7 %collective-permute-start.3 = (bf16[128,1024]{1,0:T(8,128)(2,1)}, bf16[128,1024]{1,0:T(8,128)(2,1)S(1)}, u32[]{:S(2)}, u32[]{:S(2)}) collective-permute-start(bf16[128,1024]{1,0:T(8,128)(2,1)} %pad_maximum_fusion.5), channel_id=1, source_target_pairs={{0,2},{1,6},{2,0},{3,4},{4,3},{5,7},{6,1},{7,5},{8,10},{9,14},{10,... | collective-permute-start | bytes 786440 | tf_op jit(solution)/shard_map/ppermute | solution.py:30
  72.4 20.4 %collective-permute-start.4 = (bf16[128,1024]{1,0:T(8,128)(2,1)}, bf16[128,1024]{1,0:T(8,128)(2,1)S(1)}, u32[]{:S(2)}, u32[]{:S(2)}) collective-permute-start(bf16[128,1024]{1,0:T(8,128)(2,1)} %pad_maximum_fusion.5), channel_id=1, source_target_pairs={{0,4},{1,0},{2,6},{3,2},{4,5},{5,1},{6,7},{7,3},{8,12},{9,8},{10,1... | collective-permute-start | bytes 786440 | tf_op jit(solution)/shard_map/ppermute | solution.py:30
  79.7 40.8 %all-to-all-start = ((bf16[32,32,512]{2,1,0:T(8,128)(2,1)}), bf16[32,32,512]{2,1,0:T(8,128)(2,1)S(1)}, u32[]{:S(2)}, u32[]{:S(2)}) async-start(bf16[32,32,512]{2,1,0:T(8,128)(2,1)} %get-tuple-element.18), calls=%async_computation | async-start | bytes 2097152 | tf_op jit(solution)/shard_map/all_to_all | solution.py:156
  101.3 47.1 %collective-permute-start.20 = (bf16[256,1024]{1,0:T(8,128)(2,1)}, bf16[256,1024]{1,0:T(8,128)(2,1)}, u32[]{:S(2)}, u32[]{:S(2)}) collective-permute-start(bf16[256,1024]{1,0:T(8,128)(2,1)} %get-tuple-element.23), channel_id=1, source_target_pairs={{0,24},{1,25},{2,26},{3,27},{4,28},{5,29},{6,30},{7,31},{8,16},{9,... | collective-permute-start | bytes 1572872 | tf_op jit(solution)/shard_map/ppermute | solution.py:30
  105.2 47.1 %collective-permute-start.18 = (bf16[256,1024]{1,0:T(8,128)(2,1)}, bf16[256,1024]{1,0:T(8,128)(2,1)}, u32[]{:S(2)}, u32[]{:S(2)}) collective-permute-start(bf16[256,1024]{1,0:T(8,128)(2,1)} %get-tuple-element.23), channel_id=1, source_target_pairs={{0,8},{1,9},{2,10},{3,11},{4,12},{5,13},{6,14},{7,15},{8,0},{9,1},... | collective-permute-start | bytes 1572872 | tf_op jit(solution)/shard_map/ppermute | solution.py:30
  105.2 47.0 %collective-permute-start.19 = (bf16[256,1024]{1,0:T(8,128)(2,1)}, bf16[256,1024]{1,0:T(8,128)(2,1)}, u32[]{:S(2)}, u32[]{:S(2)}) collective-permute-start(bf16[256,1024]{1,0:T(8,128)(2,1)} %get-tuple-element.22), channel_id=1, source_target_pairs={{0,16},{1,17},{2,18},{3,19},{4,20},{5,21},{6,22},{7,23},{8,24},{9,... | collective-permute-start | bytes 1572872 | tf_op jit(solution)/shard_map/ppermute | solution.py:30
  116.0 25.0 %collective-permute-start.8 = (bf16[128,512]{1,0:T(8,128)(2,1)S(1)}, bf16[128,512]{1,0:T(8,128)(2,1)S(1)}, u32[]{:S(2)}, u32[]{:S(2)}) collective-permute-start(bf16[128,512]{1,0:T(8,128)(2,1)S(1)} %get-tuple-element.11), channel_id=1, source_target_pairs={{0,1},{1,0},{2,3},{3,2},{4,5},{5,4},{6,7},{7,6},{8,9},{9,8},{10,11... | collective-permute-start | bytes 393224 | tf_op jit(solution)/shard_map/ppermute | solution.py:30
  125.6 18.2 %collective-permute-start.7 = (bf16[128,512]{1,0:T(8,128)(2,1)S(1)}, bf16[128,512]{1,0:T(8,128)(2,1)S(1)}, u32[]{:S(2)}, u32[]{:S(2)}) collective-permute-start(bf16[128,512]{1,0:T(8,128)(2,1)S(1)} %get-tuple-element.10), channel_id=1, source_target_pairs={{0,1},{1,0},{2,3},{3,2},{4,5},{5,4},{6,7},{7,6},{8,9},{9,8},{10,11... | collective-permute-start | bytes 393224 | tf_op jit(solution)/shard_map/ppermute | solution.py:30
  128.3 86.3 %all-to-all-start.3 = ((bf16[32,32,512]{2,1,0:T(8,128)(2,1)}), bf16[32,32,512]{2,1,0:T(8,128)(2,1)S(1)}, u32[]{:S(2)}, u32[]{:S(2)}) async-start(bf16[32,32,512]{2,1,0:T(8,128)(2,1)} %get-tuple-element.15), calls=%async_computation.3 | async-start | bytes 2097152 | tf_op jit(solution)/shard_map/all_to_all | solution.py:195
  152.2 17.4 %collective-permute-start.17 = (bf16[256,256]{1,0:T(8,128)(2,1)S(1)}, bf16[256,256]{1,0:T(8,128)(2,1)S(1)}, u32[]{:S(2)}, u32[]{:S(2)}) collective-permute-start(bf16[256,256]{1,0:T(8,128)(2,1)S(1)} %get-tuple-element.38), channel_id=1, source_target_pairs={{0,24},{1,25},{2,26},{3,27},{4,28},{5,29},{6,30},{7,31},{8,16},{9,... | collective-permute-start | bytes 393224 | tf_op jit(solution)/shard_map/ppermute | solution.py:30
  152.3 18.0 %collective-permute-start.16 = (bf16[256,256]{1,0:T(8,128)(2,1)S(1)}, bf16[256,256]{1,0:T(8,128)(2,1)S(1)}, u32[]{:S(2)}, u32[]{:S(2)}) collective-permute-start(bf16[256,256]{1,0:T(8,128)(2,1)S(1)} %get-tuple-element.38), channel_id=1, source_target_pairs={{0,16},{1,17},{2,18},{3,19},{4,20},{5,21},{6,22},{7,23},{8,24},{9,... | collective-permute-start | bytes 393224 | tf_op jit(solution)/shard_map/ppermute | solution.py:30
  155.2 19.3 %collective-permute-start.12 = (bf16[128,1024]{1,0:T(8,128)(2,1)S(1)}, bf16[128,1024]{1,0:T(8,128)(2,1)S(1)}, u32[]{:S(2)}, u32[]{:S(2)}) collective-permute-start(bf16[128,1024]{1,0:T(8,128)(2,1)S(1)} %get-tuple-element.25), channel_id=1, source_target_pairs={{0,3},{1,7},{2,1},{3,5},{4,2},{5,6},{6,0},{7,4},{8,11},{9,15},{10,... | collective-permute-start | bytes 786440 | tf_op jit(solution)/shard_map/ppermute | solution.py:30
  156.9 29.6 %collective-permute-start.11 = (bf16[128,1024]{1,0:T(8,128)(2,1)S(1)}, bf16[128,1024]{1,0:T(8,128)(2,1)S(1)}, u32[]{:S(2)}, u32[]{:S(2)}) collective-permute-start(bf16[128,1024]{1,0:T(8,128)(2,1)S(1)} %get-tuple-element.26), channel_id=1, source_target_pairs={{0,1},{1,5},{2,3},{3,7},{4,0},{5,4},{6,2},{7,6},{8,9},{9,13},{10,1... | collective-permute-start | bytes 786440 | tf_op jit(solution)/shard_map/ppermute | solution.py:30
  169.6 19.4 %collective-permute-start.10 = (bf16[128,1024]{1,0:T(8,128)(2,1)S(1)}, bf16[128,1024]{1,0:T(8,128)(2,1)S(1)}, u32[]{:S(2)}, u32[]{:S(2)}) collective-permute-start(bf16[128,1024]{1,0:T(8,128)(2,1)S(1)} %get-tuple-element.27), channel_id=1, source_target_pairs={{0,2},{1,6},{2,0},{3,4},{4,3},{5,7},{6,1},{7,5},{8,10},{9,14},{10,... | collective-permute-start | bytes 786440 | tf_op jit(solution)/shard_map/ppermute | solution.py:30
  170.3 18.6 %collective-permute-start.9 = (bf16[128,1024]{1,0:T(8,128)(2,1)S(1)}, bf16[128,1024]{1,0:T(8,128)(2,1)S(1)}, u32[]{:S(2)}, u32[]{:S(2)}) collective-permute-start(bf16[128,1024]{1,0:T(8,128)(2,1)S(1)} %get-tuple-element.24), channel_id=1, source_target_pairs={{0,0},{1,4},{2,2},{3,6},{4,1},{5,5},{6,3},{7,7},{8,8},{9,12},{10,1... | collective-permute-start | bytes 786440 | tf_op jit(solution)/shard_map/ppermute | solution.py:30
  171.0 21.3 %collective-permute-start.27 = (bf16[4,2,16,1024]{3,2,1,0:T(8,128)(2,1)S(1)}, bf16[4,2,16,1024]{3,2,1,0:T(8,128)(2,1)S(1)}, u32[]{:S(2)}, u32[]{:S(2)}) collective-permute-start(bf16[4,2,16,1024]{3,2,1,0:T(8,128)(2,1)S(1)} %fusion.24), channel_id=1, source_target_pairs={{0,32},{1,33},{2,34},{3,35},{4,36},{5,37},{6,38},{7,39},{8,40},{9,... | collective-permute-start | bytes 786440 | tf_op jit(solution)/shard_map/ppermute | solution.py:30
  175.2 23.7 %collective-permute-start.14 = (bf16[64,1024]{1,0:T(8,128)(2,1)S(1)}, bf16[64,1024]{1,0:T(8,128)(2,1)S(1)}, u32[]{:S(2)}, u32[]{:S(2)}) collective-permute-start(bf16[64,1024]{1,0:T(8,128)(2,1)S(1)} %copy-done.3), channel_id=1, source_target_pairs={{0,8},{1,9},{2,10},{3,11},{4,12},{5,13},{6,14},{7,15},{8,16},{9,17... | collective-permute-start | bytes 393224 | tf_op jit(solution)/shard_map/ppermute | solution.py:30
  206.6 19.9 %collective-permute-start.29 = (bf16[1,2,16,1024]{3,2,1,0:T(8,128)(2,1)S(1)}, bf16[1,2,16,1024]{3,2,1,0:T(8,128)(2,1)S(1)}, u32[]{:S(2)}, u32[]{:S(2)}) collective-permute-start(bf16[1,2,16,1024]{3,2,1,0:T(8,128)(2,1)S(1)} %fusion.35), channel_id=1, source_target_pairs={{0,128},{1,129},{2,130},{3,131},{4,132},{5,133},{6,134},{7,135},{8... | collective-permute-start | bytes 196616 | tf_op jit(solution)/shard_map/ppermute | solution.py:30
  209.4 17.1 %collective-permute-start.23 = (bf16[1,2,16,1024]{3,2,1,0:T(8,128)(2,1)S(1)}, bf16[1,2,16,1024]{3,2,1,0:T(8,128)(2,1)S(1)}, u32[]{:S(2)}, u32[]{:S(2)}) collective-permute-start(bf16[1,2,16,1024]{3,2,1,0:T(8,128)(2,1)S(1)} %fusion.34), channel_id=1, source_target_pairs={{0,128},{1,129},{2,130},{3,131},{4,132},{5,133},{6,134},{7,135},{8... | collective-permute-start | bytes 196616 | tf_op jit(solution)/shard_map/ppermute | solution.py:30
  214.6 40.8 %all-to-all-start.2 = ((bf16[32,32,512]{2,1,0:T(8,128)(2,1)}), bf16[32,32,512]{2,1,0:T(8,128)(2,1)}, u32[]{:S(2)}, u32[]{:S(2)}) async-start(bf16[32,32,512]{2,1,0:T(8,128)(2,1)} %get-tuple-element.14), calls=%async_computation.2 | async-start | bytes 2097152 | tf_op jit(solution)/shard_map/all_to_all | solution.py:195
  (18 other events, 232.6 us)

commit v2 on v1

v2 whole, which is shorter than its diff:
```python
import jax
import jax.numpy as jnp
from jax import lax
from jax.experimental import pallas as pl
from jax.experimental.pallas import tpu as pltpu
from jax.sharding import Mesh, PartitionSpec as P

CLEN = 64
NLEN = 128
HD = 128
BLK = 16
SHARDS = 32
TENSOR = 4
REPLICAS = 2
NEG_FILL = -1e30
STEPS = 4
GROUP = 2
SEQ = ("z", "y", "core")
AXES = SEQ + ("tensor", "dp")
TAIL = 8


def moved(value, where):
    pairs = []
    for s in range(SHARDS):
        for t in range(TENSOR):
            for d in range(REPLICAS):
                to = where(s, t, d)
                if to is not None:
                    pairs.append(((s * TENSOR + t) * REPLICAS + d, (to[0] * TENSOR + to[1]) * REPLICAS + to[2]))
    return lax.ppermute(value, AXES, pairs)


def to_previous(value):
    return moved(value, lambda s, t, d: (s - 1, t, d) if s > 0 else None)


def to_next(value):
    return moved(value, lambda s, t, d: (s + 1, t, d) if s + 1 < SHARDS else None)


def flip_seq(value, bits):
    return moved(value, lambda s, t, d: (s ^ bits, t, d))


def flip_tensor(value, bits):
    return moved(value, lambda s, t, d: (s, t ^ bits, d))


def flip_dp(value):
    return moved(value, lambda s, t, d: (s, t, 1 - d))


def pick(index, options):
    chosen = options[-1]
    for at in range(len(options) - 2, -1, -1):
        chosen = jnp.where(index == at, options[at], chosen)
    return chosen


def window_rows(own, after):
    half = after.shape[0]
    last = lax.broadcasted_iota(jnp.int32, (half, 1), 0) == half - 1
    return jnp.concatenate([own[-half:], jnp.where(last, own[-half - 1 : -half], after)], axis=0)


def token_rows(own, before):
    half = before.shape[0]
    last = lax.broadcasted_iota(jnp.int32, (half, 1), 0) == half - 1
    return jnp.concatenate([jnp.where(last, own[-1:], before), own[:half]], axis=0)


def split_kernel(query_ref, grad_ref, query_first_ref, grad_first_ref, grad_last_ref):
    half = query_first_ref.shape[0]
    query_first_ref[...] = query_ref[:half, :]
    grad_first_ref[...] = grad_ref[:half, :]
    grad_last_ref[...] = grad_ref[half - BLK :, :]


def split(query, grad):
    rows, width = query.shape
    vmem = pl.BlockSpec(memory_space=pltpu.VMEM)
    return pl.pallas_call(
        split_kernel,
        in_specs=[vmem] * 2,
        out_specs=[vmem] * 3,
        out_shape=[
            jax.ShapeDtypeStruct((size, width), jnp.bfloat16) for size in (rows // 2, rows // 2, rows // 2 + BLK)
        ],
        compiler_params=pltpu.CompilerParams(vmem_limit_bytes=56 * 1024 * 1024),
        cost_estimate=pl.CostEstimate(flops=0, bytes_accessed=16 * rows * width, transcendentals=0),
    )(query, grad)


def pack_kernel(target_ref, rows_ref, out_ref):
    step = pl.program_id(0)
    heads = rows_ref.shape[2] // HD
    blocks = rows_ref.shape[0] // BLK
    for at in range(blocks):
        target = target_ref[step * blocks + at]
        place = target // SHARDS
        for head in range(heads):
            pair = jnp.transpose(rows_ref[at * BLK : (at + 1) * BLK, :, head * HD : (head + 1) * HD], (1, 0, 2))
            row = 2 * BLK * head
            out_ref[place, row : row + BLK, :] = pair[0]
            out_ref[place, row + BLK : row + 2 * BLK, :] = pair[1]
        slot = jnp.full((TAIL, HD), target % SHARDS, jnp.int32)
        out_ref[place, 2 * BLK * heads :, :] = slot.astype(jnp.float32).astype(jnp.bfloat16)


def pack(target, rows):
    total, _, width = rows.shape
    out_rows = 2 * BLK * (width // HD) + TAIL
    return pl.pallas_call(
        pack_kernel,
        grid=(STEPS,),
        in_specs=[
            pl.BlockSpec(memory_space=pltpu.SMEM),
            pl.BlockSpec((total // STEPS, 2, width), lambda step: (step, 0, 0)),
        ],
        out_specs=pl.BlockSpec((SHARDS, out_rows, HD), lambda step: (0, 0, 0)),
        out_shape=jax.ShapeDtypeStruct((SHARDS, out_rows, HD), jnp.bfloat16),
        compiler_params=pltpu.CompilerParams(vmem_limit_bytes=56 * 1024 * 1024),
        cost_estimate=pl.CostEstimate(flops=0, bytes_accessed=16 * rows.size, transcendentals=0),
    )(target, rows)


def unpack_kernel(target_ref, part_ref, out_ref):
    step = pl.program_id(0)
    heads = out_ref.shape[2] // HD
    blocks = out_ref.shape[0] // BLK
    for at in range(blocks):
        source = target_ref[step * blocks + at] // SHARDS
        for head in range(heads):
            row = 2 * BLK * head
            both = part_ref[source, row : row + 2 * BLK, :].reshape(2, BLK, HD)
            out_ref[at * BLK : (at + 1) * BLK, :, head * HD : (head + 1) * HD] = jnp.transpose(both, (1, 0, 2))


def unpack(target, part):
    total, width = SHARDS * BLK, part.shape[1] // (2 * BLK) * HD
    return pl.pallas_call(
        unpack_kernel,
        grid=(STEPS,),
        in_specs=[
            pl.BlockSpec(memory_space=pltpu.SMEM),
            pl.BlockSpec(part.shape, lambda step: (0, 0, 0)),
        ],
        out_specs=pl.BlockSpec((total // STEPS, 2, width), lambda step: (step, 0, 0)),
        out_shape=jax.ShapeDtypeStruct((total, 2, width), jnp.bfloat16),
        compiler_params=pltpu.CompilerParams(vmem_limit_bytes=32 * 1024 * 1024),
        cost_estimate=pl.CostEstimate(flops=0, bytes_accessed=16 * total * width, transcendentals=0),
    )(target, part)


def attend_kernel(bias_ref, query_ref, grad_ref, kv_ref, grad_kv_ref, context_ref, grad_query_ref):
    rows = query_ref.shape[0]
    heads = query_ref.shape[1] // HD
    blocks = kv_ref.shape[0]
    keys = blocks * BLK
    scale = HD ** (-0.5)
    row = lax.broadcasted_iota(jnp.int32, (rows, 1), 0)
    second = (row >= CLEN - 1) & (row < rows - 1)
    bias = jnp.where(second, bias_ref[1:2, :], bias_ref[0:1, :])
    nt = (((1,), (1,)), ((), ()))
    tn = (((0,), (0,)), ((), ()))
    for head in range(heads):
        lanes = slice(head * HD, (head + 1) * HD)
        first, middle, last = 2 * BLK * head, 2 * BLK * head + BLK, 2 * BLK * (head + 1)
        query = query_ref[:, lanes]
        grad = grad_ref[:, lanes]
        key = kv_ref[:, first:middle, :].reshape(keys, HD)
        value = kv_ref[:, middle:last, :].reshape(keys, HD)
        scores = lax.dot_general(query, key, nt, preferred_element_type=jnp.float32) * scale + bias
        raw = jnp.exp(scores - jnp.max(scores, axis=-1, keepdims=True))
        soft = raw * (1.0 / jnp.sum(raw, axis=-1, keepdims=True))
        low = soft.astype(jnp.bfloat16)
        context = jnp.dot(low, value, preferred_element_type=jnp.float32).astype(jnp.bfloat16)
        context_ref[:, lanes] = context
        grad_weights = lax.dot_general(grad, value, nt, preferred_element_type=jnp.float32)
        delta = jnp.sum(grad.astype(jnp.float32) * context.astype(jnp.float32), axis=-1, keepdims=True)
        grad_scores = (soft * (grad_weights - delta) * scale).astype(jnp.bfloat16)
        grad_query = jnp.dot(grad_scores, key, preferred_element_type=jnp.float32)
        grad_query_ref[:, lanes] = grad_query.astype(jnp.bfloat16)
        grad_key = lax.dot_general(grad_scores, query, tn, preferred_element_type=jnp.float32)
        grad_value = lax.dot_general(low, grad, tn, preferred_element_type=jnp.float32)
        grad_kv_ref[:, first:middle, :] = grad_key.astype(jnp.bfloat16).reshape(blocks, BLK, HD)
        grad_kv_ref[:, middle:last, :] = grad_value.astype(jnp.bfloat16).reshape(blocks, BLK, HD)


def attend(bias, query, grad, kv):
    rows, width = query.shape
    blocks = kv.shape[0]
    keys = blocks * BLK
    heads = width // HD
    per_head = pl.BlockSpec((rows, GROUP * HD), lambda h: (0, h))
    block_spec = pl.BlockSpec((blocks, GROUP * 2 * BLK, HD), lambda h: (0, h, 0))
    return pl.pallas_call(
        attend_kernel,
        grid=(heads // GROUP,),
        in_specs=[pl.BlockSpec((2, keys), lambda h: (0, 0)), per_head, per_head, block_spec],
        out_specs=[block_spec, per_head, per_head],
        out_shape=[
            jax.ShapeDtypeStruct((blocks, 2 * BLK * heads, HD), jnp.bfloat16),
            jax.ShapeDtypeStruct((rows, width), jnp.bfloat16),
            jax.ShapeDtypeStruct((rows, width), jnp.bfloat16),
        ],
        compiler_params=pltpu.CompilerParams(vmem_limit_bytes=56 * 1024 * 1024),
        cost_estimate=pl.CostEstimate(
            flops=heads * 12 * rows * keys * HD,
            bytes_accessed=4 * kv.size + 8 * rows * width,
            transcendentals=heads * rows * keys,
        ),
    )(bias, query, grad, kv)


def local(queries, neighbour_kv, block_target, neighbour_count, out_weight, grad_mixed):
    seq_place = lax.axis_index(SEQ)
    tensor_place = lax.axis_index("tensor")
    dp_place = lax.axis_index("dp")
    core = seq_place % 2
    pair = (seq_place // 2) % 2
    rows, inner_dev = queries.shape[1:]
    heads_dev = inner_dev // HD

    half = rows // 2
    query_first, grad_first, grad_last = split(queries[0], grad_mixed[0])
    query_after = to_previous(query_first)
    grad_own = moved(grad_last, lambda s, t, d: (s, 2 * d + t % 2, t // 2))
    grad_after = moved(
        grad_first, lambda s, t, d: (s - 1, 2 * d + t % 2, t // 2) if s > 0 else None
    )
    packed = pack(block_target[0], neighbour_kv[0])
    packed, grad_own, grad_after, query_after = lax.optimization_barrier((packed, grad_own, grad_after, query_after))
    incoming = lax.all_to_all(packed, SEQ, split_axis=0, concat_axis=0, tiled=True)
    grad_rows = window_rows(grad_own, grad_after)
    rounds = [grad_rows] + [flip_tensor(grad_rows, bits) for bits in (1, 2, 3)]
    pair_rows = flip_seq(grad_rows, 2)
    pair_rows, rounds = lax.optimization_barrier((pair_rows, rounds))
    pair_rounds = [pair_rows] + [flip_tensor(pair_rows, bits) for bits in (1, 2, 3)]
    slot = incoming[:, -TAIL, 0].astype(jnp.int32)
    counts = lax.dynamic_slice(neighbour_count[0], (2 * seq_place,), (2,))
    live = (slot[None, :] // 16 == jnp.arange(2)[:, None]) & (slot[None, :] % 16 // 8 < counts[:, None])
    bias = jnp.where(jnp.repeat(live, BLK, axis=1), 0.0, NEG_FILL).astype(jnp.float32)

    query_rows = window_rows(queries[0], query_after)
    def column_halves(blocks):
        quarter = [pick(tensor_place ^ at, blocks) for at in range(4)]
        return [jnp.concatenate([quarter[k], quarter[2 + k]], axis=0) for k in range(2)]

    columns = column_halves(rounds)
    pair_columns = column_halves(pair_rounds)
    weight = out_weight.reshape(inner_dev, -1)
    grad_half = jnp.concatenate(columns, axis=1)
    partial_grad = lax.dot_general(
        grad_half, weight, (((1,), (1,)), ((), ())), preferred_element_type=jnp.float32
    ).reshape(2, rows, inner_dev)
    grad_own = jnp.where(dp_place == 0, partial_grad[0], partial_grad[1])
    grad_other = jnp.where(dp_place == 0, partial_grad[1], partial_grad[0]).astype(jnp.bfloat16)
    grad_context = (grad_own + flip_dp(grad_other).astype(jnp.float32)).astype(jnp.bfloat16)

    columns = [jnp.concatenate(both, axis=0) for both in zip(columns, pair_columns)]
    columns_own = jnp.where(core == 0, columns[0], columns[1])
    columns_other = flip_seq(jnp.where(core == 0, columns[1], columns[0]), 1)

    sent_back, context, grad_query = attend(bias, query_rows, grad_context, incoming)
    side = inner_dev // 2
    half_own = jnp.where(pair == 0, context[:, :side], context[:, side:])
    half_other = jnp.where(pair == 0, context[:, side:], context[:, :side])
    context_other = flip_dp(context)
    pair_own = flip_seq(half_other, 2)
    pair_other = moved(half_other, lambda s, t, d: (s ^ 2, t, 1 - d))
    sent_back, columns_own, columns_other = lax.optimization_barrier((sent_back, columns_own, columns_other))
    grad_blocks = lax.all_to_all(sent_back, SEQ, split_axis=0, concat_axis=0, tiled=True)

    def by_replica(own, other):
        return jnp.concatenate([jnp.where(dp_place == 0, own, other), jnp.where(dp_place == 0, other, own)], axis=0)

    context_both = by_replica(context, context_other)
    half_both = by_replica(half_own, jnp.where(pair == 0, context_other[:, :side], context_other[:, side:]))
    half_pair = jnp.concatenate([half_both, by_replica(pair_own, pair_other)], axis=0)
    context_group = jnp.concatenate([half_pair, flip_seq(half_pair, 1)], axis=0)
    grad_group = jnp.concatenate([columns_own, columns_other], axis=0)
    terms = lax.dot_general(context_group, grad_group, (((0,), (0,)), ((), ())), preferred_element_type=jnp.float32)
    terms, context_both = lax.optimization_barrier((terms.astype(jnp.bfloat16), context_both))
    terms = terms.reshape(side // HD, 8, HD // 8, -1)
    z = seq_place // 4
    parity = z % 2
    by_parity = terms.reshape(side // HD, 4, 2, HD // 8, -1)
    kept = jnp.where(parity == 0, by_parity[:, :, 0], by_parity[:, :, 1])
    given = jnp.where(parity == 0, by_parity[:, :, 1], by_parity[:, :, 0])
    middle = given.shape[-1] // 2
    came = jnp.concatenate(
        [
            moved(given[..., :middle], lambda s, t, d: (s + 4 if s // 4 % 2 == 0 else s - 4, t, d)),
            moved(given[..., middle:], lambda s, t, d: ((s - 4 if s // 4 % 2 == 0 else s + 4) % SHARDS, t, d)),
        ],
        axis=-1,
    )
    terms = (kept.astype(jnp.float32) + came.astype(jnp.float32)).astype(jnp.bfloat16)
    partial_out = jnp.dot(context_both, weight, preferred_element_type=jnp.float32).astype(jnp.bfloat16)
    width = partial_out.shape[1] // 2
    total = None
    for bits in range(4):
        piece = tensor_place ^ bits
        sent = lax.dynamic_slice(partial_out, (piece // 2 * rows, piece % 2 * width), (rows, width))
        came = (flip_tensor(sent, bits) if bits else sent).astype(jnp.float32)
        total = came if total is None else total + came
    total = total.astype(jnp.bfloat16)
    terms, grad_blocks, total = lax.optimization_barrier((terms, grad_blocks, total))
    out_own = moved(
        jnp.concatenate([total[:half], total[-BLK:]], axis=0), lambda s, t, d: (s, 2 * d + t % 2, t // 2)
    )
    out_before = moved(
        total[half:], lambda s, t, d: (s + 1, 2 * d + t % 2, t // 2) if s + 1 < SHARDS else None
    )
    summed = lax.dynamic_index_in_dim(terms, z // 2, axis=1, keepdims=False).astype(jnp.float32)
    for step in (2, 1, 3):
        sent = lax.dynamic_index_in_dim(terms, (z // 2 + step) % 4, axis=1, keepdims=False)
        came = moved(sent, lambda s, t, d, step=step: ((s + 8 * step) % SHARDS, t, d))
        summed = summed + came.astype(jnp.float32)
    grad_kv = unpack(block_target[0], grad_blocks)
    summed, grad_kv = lax.optimization_barrier((summed, grad_kv))
    summed, out_own, out_before = lax.optimization_barrier((summed, out_own, out_before))
    summed = summed.astype(jnp.bfloat16).reshape(side // HD, 4, HD // SHARDS, -1)
    place = 2 * pair + core
    quarters = [summed[:, at] for at in range(4)]
    received = [pick(place, quarters)] + [flip_seq(pick(place ^ bits, quarters), bits) for bits in (1, 2, 3)]
    by_pair = [jnp.concatenate([pick((2 * p + c) ^ place, received) for c in range(2)], axis=-1) for p in range(2)]
    weight_grad = jnp.concatenate(by_pair, axis=0).astype(jnp.float32)

    layer_out = token_rows(out_own, out_before)
    grad_queries = token_rows(grad_query, to_next(grad_query[half:]))

    return (layer_out[None], grad_queries[None], grad_kv[None], weight_grad)


def solution(mesh):
    fine = Mesh(mesh.devices.reshape(8, 2, 2, TENSOR, REPLICAS), AXES)
    in_specs = (
        P("dp", SEQ, "tensor"),
        P("dp", SEQ, None, "tensor"),
        P("dp", SEQ),
        P("dp", None),
        P("tensor", None, "dp"),
        P("dp", SEQ, "tensor"),
    )
    out_specs = (
        P("dp", SEQ, "tensor"),
        P("dp", SEQ, "tensor"),
        P("dp", SEQ, None, "tensor"),
        P("tensor", SEQ, "dp"),
    )
    return jax.shard_map(local, mesh=fine, in_specs=in_specs, out_specs=out_specs, check_vma=False)
```

time: 265 us -> 186 us (0.70)
  the two profiles are of different devices: /device:TPU:11 before, /device:TPU:17 now
where the time goes in v2:
time: 186 us
  starting transfers between devices  80.6 us (43%)
  waiting for transfers between devices  64.4 us (35%)
  Pallas kernels  18.1 us (10%)
  other arithmetic  11.2 us (6%)
  matrix products  7.4 us (4%)
  local copies, waits for them, and re-layouts  3.12 us (2%)
    ppermute x30, starting transfers between devices, moved(): return lax.ppermute(value, AXES, pairs)  65.1 us
    ppermute x30, waiting for transfers between devices, moved(): return lax.ppermute(value, AXES, pairs)  54.7 us
    all_to_all x1, starting transfers between devices, local(): lax.all_to_all(packed, SEQ, split_axis=0, concat_axis=0, tiled=True)  10.4 us
    all_to_all x1, waiting for transfers between devices, local(): lax.all_to_all(packed, SEQ, split_axis=0, concat_axis=0, tiled=True)  9.7 us
    pallas_call x1, Pallas kernels, attend(): pl.pallas_call(attend_kernel, grid=(heads // GROUP,), in_specs=[pl.BlockS...  8.12 us
    all_to_all x1, starting transfers between devices, local(): lax.all_to_all(sent_back, SEQ, split_axis=0, concat_axis=0, tiled=True)  5.04 us
    pallas_call x1, Pallas kernels, pack(): pl.pallas_call(pack_kernel, grid=(STEPS,), in_specs=[pl.BlockSpec(memory_...  4.92 us
  transfers between devices with their start and end apart: 32, of which 16 were waited for; matrix products, arithmetic and copies ran while one was open for 11% of the time, Pallas kernels for 9%

profile of v2, /device:TPU:17, one launch (start us, length us, event | category | flops | bytes accessed | tf_op | source)
XLA Modules:
  0.0 185.9 jit_solution(3148306590012991421)
XLA Ops:
  2.4 4.4 %collective-permute-start = (bf16[80,1024]{1,0:T(8,128)(2,1)}, bf16[80,1024]{1,0:T(8,128)(2,1)S(1)}, u32[]{:S(2)}, u32[]{:S(2)}) collective-permute-start(bf16[80,1024]{1,0:T(8,128)(2,1)} %get-tuple-element.32), channel_id=1, source_target_pairs={{0,0},{1,4},{2,2},{3,6},{4,1},{5,5},{6,3},{7,7},{8,8},{9,12},{10,1... | collective-permute-start | bytes 491528 | tf_op jit(solution)/shard_map/ppermute | solution.py:31
  6.9 5.6 %collective-permute-start.1 = (bf16[64,1024]{1,0:T(8,128)(2,1)}, bf16[64,1024]{1,0:T(8,128)(2,1)S(1)}, u32[]{:S(2)}, u32[]{:S(2)}) collective-permute-start(bf16[64,1024]{1,0:T(8,128)(2,1)} %get-tuple-element.33), channel_id=1, source_target_pairs={{8,0},{9,4},{10,2},{11,6},{12,1},{13,5},{14,3},{15,7},{16,8},{17,1... | collective-permute-start | bytes 393224 | tf_op jit(solution)/shard_map/ppermute | solution.py:31
  14.4 4.9 %shard_map.93 = bf16[32,264,128]{2,1,0:T(8,128)(2,1)} custom-call(s32[32]{0:T(128)} %bitcast.45, bf16[512,2,1024]{2,1,0:T(2,128)(2,1)} %bitcast.47), custom_call_target="tpu_custom_call" | custom-call | bytes 16777216 | tf_op jit(solution)/shard_map/pallas_call | solution.py:114
  19.3 10.4 %all-to-all-start = ((bf16[32,264,128]{2,1,0:T(8,128)(2,1)}), bf16[32,264,128]{2,1,0:T(8,128)(2,1)}, u32[]{:S(2)}, u32[]{:S(2)}) async-start(bf16[32,264,128]{2,1,0:T(8,128)(2,1)} %shard_map.93), calls=%async_computation | async-start | bytes 4325376 | tf_op jit(solution)/shard_map/all_to_all | solution.py:235
  32.6 2.6 %collective-permute-start.6 = (bf16[128,1024]{1,0:T(8,128)(2,1)S(1)}, bf16[128,1024]{1,0:T(8,128)(2,1)S(1)}, u32[]{:S(2)}, u32[]{:S(2)}) collective-permute-start(bf16[128,1024]{1,0:T(8,128)(2,1)S(1)} %pad_maximum_fusion.5), channel_id=1, source_target_pairs={{0,6},{1,7},{2,4},{3,5},{4,2},{5,3},{6,0},{7,1},{8,14},{9,15},{10,... | collective-permute-start | bytes 786440 | tf_op jit(solution)/shard_map/ppermute | solution.py:31
  36.2 10.1 %collective-permute-done.3 = bf16[128,1024]{1,0:T(8,128)(2,1)S(1)} collective-permute-done((bf16[128,1024]{1,0:T(8,128)(2,1)S(1)}, bf16[128,1024]{1,0:T(8,128)(2,1)S(1)}, u32[]{:S(2)}, u32[]{:S(2)}) %collective-permute-start.3) | collective-permute-done | bytes 262176 | tf_op jit(solution)/shard_map/ppermute | solution.py:31
  51.4 3.5 %fusion.7 = f32[256,1024]{1,0:T(8,128)S(1)} fusion(bf16[1024,2048]{1,0:T(8,128)(2,1)} %bitcast.55, bf16[128,1024]{1,0:T(8,128)(2,1)S(1)} %get-tuple-element.86, bf16[128,1024]{1,0:T(8,128)(2,1)S(1)} %get-tuple-element.87, bf16[128,1024]{1,0:T(8,128)(2,1)S(1)} %get-tuple-element.88, bf16[128,1024]{1,0:T(8,128)(2,1)S(1)} %get-tuple-element.85), kind=kOutput, calls=%fused_computation.6 | convolution fusion | flops 1077936128 | bytes 6291456 | tf_op jit(solution)/shard_map/dot_general | solution.py:255
  56.4 3.6 %collective-permute-done.13 = bf16[128,1024]{1,0:T(8,128)(2,1)S(1)} collective-permute-done((bf16[128,1024]{1,0:T(8,128)(2,1)S(1)}, bf16[128,1024]{1,0:T(8,128)(2,1)S(1)}, u32[]{:S(2)}, u32[]{:S(2)}) %collective-permute-start.13) | collective-permute-done | bytes 262176 | tf_op jit(solution)/shard_map/ppermute | solution.py:31
  60.0 3.4 %collective-permute-done.14 = bf16[128,1024]{1,0:T(8,128)(2,1)S(1)} collective-permute-done((bf16[128,1024]{1,0:T(8,128)(2,1)S(1)}, bf16[128,1024]{1,0:T(8,128)(2,1)S(1)}, u32[]{:S(2)}, u32[]{:S(2)}) %collective-permute-start.14) | collective-permute-done | bytes 262176 | tf_op jit(solution)/shard_map/ppermute | solution.py:31
  67.3 3.4 %collective-permute-done.7 = bf16[128,1024]{1,0:T(8,128)(2,1)S(1)} collective-permute-done((bf16[128,1024]{1,0:T(8,128)(2,1)S(1)}, bf16[128,1024]{1,0:T(8,128)(2,1)S(1)}, u32[]{:S(2)}, u32[]{:S(2)}) %collective-permute-start.7) | collective-permute-done | bytes 262176 | tf_op jit(solution)/shard_map/ppermute | solution.py:31
  71.5 9.7 %all-to-all-done.kv_ref = bf16[32,264,128]{2,1,0:T(8,128)(2,1)} async-done(((bf16[32,264,128]{2,1,0:T(8,128)(2,1)}), bf16[32,264,128]{2,1,0:T(8,128)(2,1)}, u32[]{:S(2)}, u32[]{:S(2)}) %all-to-all-start) | async-done | bytes 2162720 | tf_op jit(solution)/shard_map/all_to_all | solution.py:235
  83.6 8.1 %shard_map.95 = (bf16[32,256,128]{2,1,0:T(8,128)(2,1)}, bf16[128,1024]{1,0:T(8,128)(2,1)}, bf16[128,1024]{1,0:T(8,128)(2,1)}) custom-call(f32[2,512]{1,0:T(2,128)} %select_n.538.bias_ref, bf16[128,1024]{1,0:T(8,128)(2,1)} %pad_maximum_fusion.4.query_ref, bf16[128,1024]{1,0:T(8,128)(2,1)} %add_convert_fusion.1.grad_ref, bf16[32,264,128]{2,1,0:T(8,128)(2,1)} %all-to-all-done.kv_ref), custom_call_target="tpu_custom_call" | custom-call | flops 805306368 | bytes 5373952 | tf_op jit(solution)/shard_map/pallas_call | solution.py:198
  91.7 5.0 %all-to-all-start.1 = ((bf16[32,256,128]{2,1,0:T(8,128)(2,1)}), bf16[32,256,128]{2,1,0:T(8,128)(2,1)S(1)}, u32[]{:S(2)}, u32[]{:S(2)}) async-start(bf16[32,256,128]{2,1,0:T(8,128)(2,1)} %get-tuple-element.49), calls=%async_computation.1 | async-start | bytes 4194304 | tf_op jit(solution)/shard_map/all_to_all | solution.py:274
  96.8 4.0 %collective-permute-done.8 = bf16[128,1024]{1,0:T(8,128)(2,1)S(1)} collective-permute-done((bf16[128,1024]{1,0:T(8,128)(2,1)}, bf16[128,1024]{1,0:T(8,128)(2,1)S(1)}, u32[]{:S(2)}, u32[]{:S(2)}) %collective-permute-start.8) | collective-permute-done | bytes 262176 | tf_op jit(solution)/shard_map/ppermute | solution.py:31
  109.9 4.3 %collective-permute-start.11 = (bf16[512,512]{1,0:T(8,128)(2,1)S(1)}, bf16[512,512]{1,0:T(8,128)(2,1)S(1)}, u32[]{:S(2)}, u32[]{:S(2)}) collective-permute-start(bf16[512,512]{1,0:T(8,128)(2,1)S(1)} %pad_maximum_fusion.2), channel_id=1, source_target_pairs={{0,8},{1,9},{2,10},{3,11},{4,12},{5,13},{6,14},{7,15},{8,0},{9,1},... | collective-permute-start | bytes 1572872 | tf_op jit(solution)/shard_map/ppermute | solution.py:31
  115.8 2.7 %fusion.4 = bf16[512,1024]{1,0:T(8,128)(2,1)S(1)} fusion(bf16[1024,512]{1,0:T(8,128)(2,1)S(1)} %constant_dynamic-update-slice_fusion, bf16[512,1024]{1,0:T(8,128)(2,1)} %collective-permute-done.15, bf16[512,1024]{1,0:T(8,128)(2,1)S(1)} %copy-done.3), kind=kOutput, calls=%fused_computation.5 | convolution fusion | flops 1078460416 | bytes 4194304 | tf_op jit(solution)/shard_map/dot_general | solution.py:284
  121.1 2.9 %collective-permute-start.19 = (bf16[128,1024]{1,0:T(8,128)(2,1)S(1)}, bf16[128,1024]{1,0:T(8,128)(2,1)S(1)}, u32[]{:S(2)}, u32[]{:S(2)}) collective-permute-start(bf16[128,1024]{1,0:T(8,128)(2,1)S(1)} %get-tuple-element.78), channel_id=1, source_target_pairs={{0,4},{1,5},{2,6},{3,7},{4,0},{5,1},{6,2},{7,3},{8,12},{9,13},{10,... | collective-permute-start | bytes 786440 | tf_op jit(solution)/shard_map/ppermute | solution.py:31
  127.5 6.0 %collective-permute-start.26 = (bf16[64,1024]{1,0:T(8,128)(2,1)}, bf16[64,1024]{1,0:T(8,128)(2,1)S(1)}, u32[]{:S(2)}, u32[]{:S(2)}) collective-permute-start(bf16[64,1024]{1,0:T(8,128)(2,1)} %get-tuple-element.96), channel_id=1, source_target_pairs={{0,8},{1,9},{2,10},{3,11},{4,12},{5,13},{6,14},{7,15},{8,16},{9,17... | collective-permute-start | bytes 393224 | tf_op jit(solution)/shard_map/ppermute | solution.py:31
  138.0 11.6 %collective-permute-done.16 = bf16[4,4,16,512]{3,0,2,1:T(4,128)(2,1)S(1)} collective-permute-done((bf16[4,4,16,512]{3,0,2,1:T(4,128)(2,1)S(1)}, bf16[4,4,16,512]{3,0,2,1:T(4,128)(2,1)S(1)}, u32[]{:S(2)}, u32[]{:S(2)}) %collective-permute-start.16) | collective-permute-done | bytes 262176 | tf_op jit(solution)/shard_map/ppermute | solution.py:31
  151.9 3.2 %collective-permute-start.21 = (bf16[4,16,1024]{2,0,1:T(4,128)(2,1)S(1)}, bf16[4,16,1024]{2,0,1:T(4,128)(2,1)S(1)}, u32[]{:S(2)}, u32[]{:S(2)}) collective-permute-start(bf16[4,16,1024]{2,0,1:T(4,128)(2,1)S(1)} %get-tuple-element.89), channel_id=1, source_target_pairs={{0,128},{1,129},{2,130},{3,131},{4,132},{5,133},{6,134},{7,135},{8... | collective-permute-start | bytes 393224 | tf_op jit(solution)/shard_map/ppermute | solution.py:31
  158.7 4.5 %collective-permute-start.24 = (bf16[80,1024]{1,0:T(8,128)(2,1)S(1)}, bf16[80,1024]{1,0:T(8,128)(2,1)S(1)}, u32[]{:S(2)}, u32[]{:S(2)}) collective-permute-start(bf16[80,1024]{1,0:T(8,128)(2,1)S(1)} %pad_maximum_fusion.6), channel_id=1, source_target_pairs={{0,0},{1,4},{2,2},{3,6},{4,1},{5,5},{6,3},{7,7},{8,8},{9,12},{10,1... | collective-permute-start | bytes 491528 | tf_op jit(solution)/shard_map/ppermute | solution.py:31
  163.3 3.3 %shard_map.96 = bf16[512,2,1024]{2,1,0:T(2,128)(2,1)} custom-call(s32[32]{0:T(128)S(1)} %bitcast.46, bf16[32,256,128]{2,1,0:T(8,128)(2,1)S(1)} %all-to-all-done.1.part_ref), custom_call_target="tpu_custom_call" | custom-call | bytes 8388608 | tf_op jit(solution)/shard_map/pallas_call | solution.py:142
  166.5 6.1 %collective-permute-start.25 = (bf16[64,1024]{1,0:T(8,128)(2,1)S(1)}, bf16[64,1024]{1,0:T(8,128)(2,1)S(1)}, u32[]{:S(2)}, u32[]{:S(2)}) collective-permute-start(bf16[64,1024]{1,0:T(8,128)(2,1)S(1)} %get-tuple-element.98), channel_id=1, source_target_pairs={{0,8},{1,12},{2,10},{3,14},{4,9},{5,13},{6,11},{7,15},{8,16},{9,20... | collective-permute-start | bytes 393224 | tf_op jit(solution)/shard_map/ppermute | solution.py:31
  172.8 3.9 %collective-permute-done.25 = bf16[64,1024]{1,0:T(8,128)(2,1)S(1)} collective-permute-done((bf16[64,1024]{1,0:T(8,128)(2,1)S(1)}, bf16[64,1024]{1,0:T(8,128)(2,1)S(1)}, u32[]{:S(2)}, u32[]{:S(2)}) %collective-permute-start.25) | collective-permute-done | bytes 131104 | tf_op jit(solution)/shard_map/ppermute | solution.py:31
  (113 shorter events, 57.4 us)
Async XLA Ops:
  2.4 16.9 %collective-permute-start = (bf16[80,1024]{1,0:T(8,128)(2,1)}, bf16[80,1024]{1,0:T(8,128)(2,1)S(1)}, u32[]{:S(2)}, u32[]{:S(2)}) collective-permute-start(bf16[80,1024]{1,0:T(8,128)(2,1)} %get-tuple-element.32), channel_id=1, source_target_pairs={{0,0},{1,4},{2,2},{3,6},{4,1},{5,5},{6,3},{7,7},{8,8},{9,12},{10,1... | collective-permute-start | bytes 491528 | tf_op jit(solution)/shard_map/ppermute | solution.py:31
  6.9 12.5 %collective-permute-start.1 = (bf16[64,1024]{1,0:T(8,128)(2,1)}, bf16[64,1024]{1,0:T(8,128)(2,1)S(1)}, u32[]{:S(2)}, u32[]{:S(2)}) collective-permute-start(bf16[64,1024]{1,0:T(8,128)(2,1)} %get-tuple-element.33), channel_id=1, source_target_pairs={{8,0},{9,4},{10,2},{11,6},{12,1},{13,5},{14,3},{15,7},{16,8},{17,1... | collective-permute-start | bytes 393224 | tf_op jit(solution)/shard_map/ppermute | solution.py:31
  19.3 61.9 %all-to-all-start = ((bf16[32,264,128]{2,1,0:T(8,128)(2,1)}), bf16[32,264,128]{2,1,0:T(8,128)(2,1)}, u32[]{:S(2)}, u32[]{:S(2)}) async-start(bf16[32,264,128]{2,1,0:T(8,128)(2,1)} %shard_map.93), calls=%async_computation | async-start | bytes 4325376 | tf_op jit(solution)/shard_map/all_to_all | solution.py:235
  29.9 16.3 %collective-permute-start.3 = (bf16[128,1024]{1,0:T(8,128)(2,1)S(1)}, bf16[128,1024]{1,0:T(8,128)(2,1)S(1)}, u32[]{:S(2)}, u32[]{:S(2)}) collective-permute-start(bf16[128,1024]{1,0:T(8,128)(2,1)S(1)} %pad_maximum_fusion.5), channel_id=1, source_target_pairs={{0,16},{1,17},{2,18},{3,19},{4,20},{5,21},{6,22},{7,23},{8,24},{9,... | collective-permute-start | bytes 786440 | tf_op jit(solution)/shard_map/ppermute | solution.py:31
  31.4 14.8 %collective-permute-start.4 = (bf16[128,1024]{1,0:T(8,128)(2,1)S(1)}, bf16[128,1024]{1,0:T(8,128)(2,1)S(1)}, u32[]{:S(2)}, u32[]{:S(2)}) collective-permute-start(bf16[128,1024]{1,0:T(8,128)(2,1)S(1)} %pad_maximum_fusion.5), channel_id=1, source_target_pairs={{0,2},{1,3},{2,0},{3,1},{4,6},{5,7},{6,4},{7,5},{8,10},{9,11},{10,... | collective-permute-start | bytes 786440 | tf_op jit(solution)/shard_map/ppermute | solution.py:31
  32.6 13.6 %collective-permute-start.5 = (bf16[128,1024]{1,0:T(8,128)(2,1)S(1)}, bf16[128,1024]{1,0:T(8,128)(2,1)S(1)}, u32[]{:S(2)}, u32[]{:S(2)}) collective-permute-start(bf16[128,1024]{1,0:T(8,128)(2,1)S(1)} %pad_maximum_fusion.5), channel_id=1, source_target_pairs={{0,4},{1,5},{2,6},{3,7},{4,0},{5,1},{6,2},{7,3},{8,12},{9,13},{10,... | collective-permute-start | bytes 786440 | tf_op jit(solution)/shard_map/ppermute | solution.py:31
  32.6 14.8 %collective-permute-start.6 = (bf16[128,1024]{1,0:T(8,128)(2,1)S(1)}, bf16[128,1024]{1,0:T(8,128)(2,1)S(1)}, u32[]{:S(2)}, u32[]{:S(2)}) collective-permute-start(bf16[128,1024]{1,0:T(8,128)(2,1)S(1)} %pad_maximum_fusion.5), channel_id=1, source_target_pairs={{0,6},{1,7},{2,4},{3,5},{4,2},{5,3},{6,0},{7,1},{8,14},{9,15},{10,... | collective-permute-start | bytes 786440 | tf_op jit(solution)/shard_map/ppermute | solution.py:31
  47.5 8.9 %collective-permute-start.12 = (bf16[128,1024]{1,0:T(8,128)(2,1)S(1)}, bf16[128,1024]{1,0:T(8,128)(2,1)S(1)}, u32[]{:S(2)}, u32[]{:S(2)}) collective-permute-start(bf16[128,1024]{1,0:T(8,128)(2,1)S(1)} %collective-permute-done.3), channel_id=1, source_target_pairs={{0,2},{1,3},{2,0},{3,1},{4,6},{5,7},{6,4},{7,5},{8,10},{9,11},{10,... | collective-permute-start | bytes 786440 | tf_op jit(solution)/shard_map/ppermute | solution.py:31
  47.5 12.5 %collective-permute-start.13 = (bf16[128,1024]{1,0:T(8,128)(2,1)S(1)}, bf16[128,1024]{1,0:T(8,128)(2,1)S(1)}, u32[]{:S(2)}, u32[]{:S(2)}) collective-permute-start(bf16[128,1024]{1,0:T(8,128)(2,1)S(1)} %collective-permute-done.3), channel_id=1, source_target_pairs={{0,4},{1,5},{2,6},{3,7},{4,0},{5,1},{6,2},{7,3},{8,12},{9,13},{10,... | collective-permute-start | bytes 786440 | tf_op jit(solution)/shard_map/ppermute | solution.py:31
  50.0 13.5 %collective-permute-start.14 = (bf16[128,1024]{1,0:T(8,128)(2,1)S(1)}, bf16[128,1024]{1,0:T(8,128)(2,1)S(1)}, u32[]{:S(2)}, u32[]{:S(2)}) collective-permute-start(bf16[128,1024]{1,0:T(8,128)(2,1)S(1)} %collective-permute-done.3), channel_id=1, source_target_pairs={{0,6},{1,7},{2,4},{3,5},{4,2},{5,3},{6,0},{7,1},{8,14},{9,15},{10,... | collective-permute-start | bytes 786440 | tf_op jit(solution)/shard_map/ppermute | solution.py:31
  55.0 15.7 %collective-permute-start.7 = (bf16[128,1024]{1,0:T(8,128)(2,1)S(1)}, bf16[128,1024]{1,0:T(8,128)(2,1)S(1)}, u32[]{:S(2)}, u32[]{:S(2)}) collective-permute-start(bf16[128,1024]{1,0:T(8,128)(2,1)S(1)} %select_convert_fusion), channel_id=1, source_target_pairs={{0,1},{1,0},{2,3},{3,2},{4,5},{5,4},{6,7},{7,6},{8,9},{9,8},{10,11... | collective-permute-start | bytes 786440 | tf_op jit(solution)/shard_map/ppermute | solution.py:31
  65.2 26.4 %collective-permute-start.15 = (bf16[512,1024]{1,0:T(8,128)(2,1)S(1)}, bf16[512,1024]{1,0:T(8,128)(2,1)}, u32[]{:S(2)}, u32[]{:S(2)}) collective-permute-start(bf16[512,1024]{1,0:T(8,128)(2,1)S(1)} %get-tuple-element.74), channel_id=1, source_target_pairs={{0,8},{1,9},{2,10},{3,11},{4,12},{5,13},{6,14},{7,15},{8,0},{9,1},... | collective-permute-start | bytes 3145736 | tf_op jit(solution)/shard_map/ppermute | solution.py:31
  91.7 9.1 %collective-permute-start.8 = (bf16[128,1024]{1,0:T(8,128)(2,1)}, bf16[128,1024]{1,0:T(8,128)(2,1)S(1)}, u32[]{:S(2)}, u32[]{:S(2)}) collective-permute-start(bf16[128,1024]{1,0:T(8,128)(2,1)} %get-tuple-element.43), channel_id=1, source_target_pairs={{0,1},{1,0},{2,3},{3,2},{4,5},{5,4},{6,7},{7,6},{8,9},{9,8},{10,11... | collective-permute-start | bytes 786440 | tf_op jit(solution)/shard_map/ppermute | solution.py:31
  91.7 60.0 %all-to-all-start.1 = ((bf16[32,256,128]{2,1,0:T(8,128)(2,1)}), bf16[32,256,128]{2,1,0:T(8,128)(2,1)S(1)}, u32[]{:S(2)}, u32[]{:S(2)}) async-start(bf16[32,256,128]{2,1,0:T(8,128)(2,1)} %get-tuple-element.49), calls=%async_computation.1 | async-start | bytes 4194304 | tf_op jit(solution)/shard_map/all_to_all | solution.py:274
  121.1 14.6 %collective-permute-start.19 = (bf16[128,1024]{1,0:T(8,128)(2,1)S(1)}, bf16[128,1024]{1,0:T(8,128)(2,1)S(1)}, u32[]{:S(2)}, u32[]{:S(2)}) collective-permute-start(bf16[128,1024]{1,0:T(8,128)(2,1)S(1)} %get-tuple-element.78), channel_id=1, source_target_pairs={{0,4},{1,5},{2,6},{3,7},{4,0},{5,1},{6,2},{7,3},{8,12},{9,13},{10,... | collective-permute-start | bytes 786440 | tf_op jit(solution)/shard_map/ppermute | solution.py:31
  124.1 13.7 %collective-permute-start.20 = (bf16[128,1024]{1,0:T(8,128)(2,1)S(1)}, bf16[128,1024]{1,0:T(8,128)(2,1)S(1)}, u32[]{:S(2)}, u32[]{:S(2)}) collective-permute-start(bf16[128,1024]{1,0:T(8,128)(2,1)S(1)} %get-tuple-element.77), channel_id=1, source_target_pairs={{0,6},{1,7},{2,4},{3,5},{4,2},{5,3},{6,0},{7,1},{8,14},{9,15},{10,... | collective-permute-start | bytes 786440 | tf_op jit(solution)/shard_map/ppermute | solution.py:31
  125.1 24.5 %collective-permute-start.16 = (bf16[4,4,16,512]{3,0,2,1:T(4,128)(2,1)S(1)}, bf16[4,4,16,512]{3,0,2,1:T(4,128)(2,1)S(1)}, u32[]{:S(2)}, u32[]{:S(2)}) collective-permute-start(bf16[4,4,16,512]{3,0,2,1:T(4,128)(2,1)S(1)} %get-tuple-element.92), channel_id=1, source_target_pairs={{0,32},{1,33},{2,34},{3,35},{4,36},{5,37},{6,38},{7,39},{8,40},{9,... | collective-permute-start | bytes 786440 | tf_op jit(solution)/shard_map/ppermute | solution.py:31
  127.5 23.4 %collective-permute-start.17 = (bf16[4,4,16,512]{3,0,2,1:T(4,128)(2,1)S(1)}, bf16[4,4,16,512]{3,0,2,1:T(4,128)(2,1)S(1)}, u32[]{:S(2)}, u32[]{:S(2)}) collective-permute-start(bf16[4,4,16,512]{3,0,2,1:T(4,128)(2,1)S(1)} %get-tuple-element.93), channel_id=1, source_target_pairs={{0,224},{1,225},{2,226},{3,227},{4,228},{5,229},{6,230},{7,231},{8... | collective-permute-start | bytes 786440 | tf_op jit(solution)/shard_map/ppermute | solution.py:31
  127.5 53.9 %collective-permute-start.26 = (bf16[64,1024]{1,0:T(8,128)(2,1)}, bf16[64,1024]{1,0:T(8,128)(2,1)S(1)}, u32[]{:S(2)}, u32[]{:S(2)}) collective-permute-start(bf16[64,1024]{1,0:T(8,128)(2,1)} %get-tuple-element.96), channel_id=1, source_target_pairs={{0,8},{1,9},{2,10},{3,11},{4,12},{5,13},{6,14},{7,15},{8,16},{9,17... | collective-permute-start | bytes 393224 | tf_op jit(solution)/shard_map/ppermute | solution.py:31
  151.9 14.6 %collective-permute-start.21 = (bf16[4,16,1024]{2,0,1:T(4,128)(2,1)S(1)}, bf16[4,16,1024]{2,0,1:T(4,128)(2,1)S(1)}, u32[]{:S(2)}, u32[]{:S(2)}) collective-permute-start(bf16[4,16,1024]{2,0,1:T(4,128)(2,1)S(1)} %get-tuple-element.89), channel_id=1, source_target_pairs={{0,128},{1,129},{2,130},{3,131},{4,132},{5,133},{6,134},{7,135},{8... | collective-permute-start | bytes 393224 | tf_op jit(solution)/shard_map/ppermute | solution.py:31
  155.1 17.6 %collective-permute-start.22 = (bf16[4,16,1024]{2,0,1:T(4,128)(2,1)S(1)}, bf16[4,16,1024]{2,0,1:T(4,128)(2,1)S(1)}, u32[]{:S(2)}, u32[]{:S(2)}) collective-permute-start(bf16[4,16,1024]{2,0,1:T(4,128)(2,1)S(1)} %get-tuple-element.91), channel_id=1, source_target_pairs={{0,64},{1,65},{2,66},{3,67},{4,68},{5,69},{6,70},{7,71},{8,72},{9,... | collective-permute-start | bytes 393224 | tf_op jit(solution)/shard_map/ppermute | solution.py:31
  156.1 16.6 %collective-permute-start.23 = (bf16[4,16,1024]{2,0,1:T(4,128)(2,1)S(1)}, bf16[4,16,1024]{2,0,1:T(4,128)(2,1)S(1)}, u32[]{:S(2)}, u32[]{:S(2)}) collective-permute-start(bf16[4,16,1024]{2,0,1:T(4,128)(2,1)S(1)} %get-tuple-element.90), channel_id=1, source_target_pairs={{0,192},{1,193},{2,194},{3,195},{4,196},{5,197},{6,198},{7,199},{8... | collective-permute-start | bytes 393224 | tf_op jit(solution)/shard_map/ppermute | solution.py:31
  158.7 18.0 %collective-permute-start.24 = (bf16[80,1024]{1,0:T(8,128)(2,1)S(1)}, bf16[80,1024]{1,0:T(8,128)(2,1)S(1)}, u32[]{:S(2)}, u32[]{:S(2)}) collective-permute-start(bf16[80,1024]{1,0:T(8,128)(2,1)S(1)} %pad_maximum_fusion.6), channel_id=1, source_target_pairs={{0,0},{1,4},{2,2},{3,6},{4,1},{5,5},{6,3},{7,7},{8,8},{9,12},{10,1... | collective-permute-start | bytes 491528 | tf_op jit(solution)/shard_map/ppermute | solution.py:31
  166.5 10.2 %collective-permute-start.25 = (bf16[64,1024]{1,0:T(8,128)(2,1)S(1)}, bf16[64,1024]{1,0:T(8,128)(2,1)S(1)}, u32[]{:S(2)}, u32[]{:S(2)}) collective-permute-start(bf16[64,1024]{1,0:T(8,128)(2,1)S(1)} %get-tuple-element.98), channel_id=1, source_target_pairs={{0,8},{1,12},{2,10},{3,14},{4,9},{5,13},{6,11},{7,15},{8,16},{9,20... | collective-permute-start | bytes 393224 | tf_op jit(solution)/shard_map/ppermute | solution.py:31
  (16 other events, 154.0 us)

commit v3 on v2

--- a/solution.py
+++ b/solution.py
@@ -153,7 +153,7 @@
     )(target, part)
 
 
-def attend_kernel(bias_ref, query_ref, grad_ref, kv_ref, grad_kv_ref, context_ref, grad_query_ref):
+def attend_kernel(count_ref, slot_ref, query_ref, grad_ref, kv_ref, grad_kv_ref, context_ref, grad_query_ref):
     rows = query_ref.shape[0]
     heads = query_ref.shape[1] // HD
     blocks = kv_ref.shape[0]
@@ -161,7 +161,14 @@
     scale = HD ** (-0.5)
     row = lax.broadcasted_iota(jnp.int32, (rows, 1), 0)
     second = (row >= CLEN - 1) & (row < rows - 1)
-    bias = jnp.where(second, bias_ref[1:2, :], bias_ref[0:1, :])
+    block = lax.broadcasted_iota(jnp.int32, (blocks, keys), 0)
+    own = (lax.broadcasted_iota(jnp.int32, (blocks, keys), 1) >> 4) == block
+    spread = jnp.where(own, 1.0, 0.0).astype(jnp.bfloat16)
+    slot = lax.dot_general(slot_ref[...], spread, (((0,), (0,)), ((), ())), preferred_element_type=jnp.float32)
+    low_slot = jnp.where(second, 16, 0)
+    high_slot = low_slot + 8 * jnp.where(second, count_ref[1], count_ref[0])
+    live = (slot >= low_slot.astype(jnp.float32)) & (slot < high_slot.astype(jnp.float32))
+    bias = jnp.where(live, 0.0, NEG_FILL)
     nt = (((1,), (1,)), ((), ()))
     tn = (((0,), (0,)), ((), ()))
     for head in range(heads):
@@ -188,7 +195,7 @@
         grad_kv_ref[:, middle:last, :] = grad_value.astype(jnp.bfloat16).reshape(blocks, BLK, HD)
 
 
-def attend(bias, query, grad, kv):
+def attend(counts, slots, query, grad, kv):
     rows, width = query.shape
     blocks = kv.shape[0]
     keys = blocks * BLK
@@ -198,7 +205,13 @@
     return pl.pallas_call(
         attend_kernel,
         grid=(heads // GROUP,),
-        in_specs=[pl.BlockSpec((2, keys), lambda h: (0, 0)), per_head, per_head, block_spec],
+        in_specs=[
+            pl.BlockSpec(memory_space=pltpu.SMEM),
+            pl.BlockSpec(slots.shape, lambda h: (0, 0)),
+            per_head,
+            per_head,
+            block_spec,
+        ],
         out_specs=[block_spec, per_head, per_head],
         out_shape=[
             jax.ShapeDtypeStruct((blocks, 2 * BLK * heads, HD), jnp.bfloat16),
@@ -211,7 +224,7 @@
             bytes_accessed=4 * kv.size + 8 * rows * width,
             transcendentals=heads * rows * keys,
         ),
-    )(bias, query, grad, kv)
+    )(counts, slots, query, grad, kv)
 
 
 def local(queries, neighbour_kv, block_target, neighbour_count, out_weight, grad_mixed):
@@ -238,10 +251,8 @@
     pair_rows = flip_seq(grad_rows, 2)
     pair_rows, rounds = lax.optimization_barrier((pair_rows, rounds))
     pair_rounds = [pair_rows] + [flip_tensor(pair_rows, bits) for bits in (1, 2, 3)]
-    slot = incoming[:, -TAIL, 0].astype(jnp.int32)
+    slots = incoming[:, -TAIL, :]
     counts = lax.dynamic_slice(neighbour_count[0], (2 * seq_place,), (2,))
-    live = (slot[None, :] // 16 == jnp.arange(2)[:, None]) & (slot[None, :] % 16 // 8 < counts[:, None])
-    bias = jnp.where(jnp.repeat(live, BLK, axis=1), 0.0, NEG_FILL).astype(jnp.float32)
 
     query_rows = window_rows(queries[0], query_after)
     def column_halves(blocks):
@@ -263,7 +274,7 @@
     columns_own = jnp.where(core == 0, columns[0], columns[1])
     columns_other = flip_seq(jnp.where(core == 0, columns[1], columns[0]), 1)
 
-    sent_back, context, grad_query = attend(bias, query_rows, grad_context, incoming)
+    sent_back, context, grad_query = attend(counts, slots, query_rows, grad_context, incoming)
     side = inner_dev // 2
     half_own = jnp.where(pair == 0, context[:, :side], context[:, side:])
     half_other = jnp.where(pair == 0, context[:, side:], context[:, :side])

time: 186 us -> 186 us (level)
  no operation moved by 1% of the time
where the time goes in v3:
time: 186 us; the launch traced here: 185 us
  starting transfers between devices  80.5 us (43%)
  waiting for transfers between devices  63.9 us (34%)
  Pallas kernels  18.4 us (10%)
  other arithmetic  9.57 us (5%)
  matrix products  7.4 us (4%)
  local copies, waits for them, and re-layouts  4.4 us (2%)
    ppermute x30, starting transfers between devices, moved(): return lax.ppermute(value, AXES, pairs)  65.1 us
    ppermute x30, waiting for transfers between devices, moved(): return lax.ppermute(value, AXES, pairs)  54.2 us
    all_to_all x1, starting transfers between devices, local(): lax.all_to_all(packed, SEQ, split_axis=0, concat_axis=0, tiled=True)  10.4 us
    all_to_all x1, waiting for transfers between devices, local(): lax.all_to_all(packed, SEQ, split_axis=0, concat_axis=0, tiled=True)  9.7 us
    pallas_call x1, Pallas kernels, attend(): pl.pallas_call(attend_kernel, grid=(heads // GROUP,), in_specs=[pl.BlockS...  8.42 us
    all_to_all x1, starting transfers between devices, local(): lax.all_to_all(sent_back, SEQ, split_axis=0, concat_axis=0, tiled=True)  5.02 us
    pallas_call x1, Pallas kernels, pack(): pl.pallas_call(pack_kernel, grid=(STEPS,), in_specs=[pl.BlockSpec(memory_...  4.93 us
  transfers between devices with their start and end apart: 32, of which 16 were waited for; matrix products, arithmetic and copies ran while one was open for 11% of the time, Pallas kernels for 9%

profile of v3, /device:TPU:17, one launch (start us, length us, event | category | flops | bytes accessed | tf_op | source)
XLA Modules:
  0.0 185.3 jit_solution(12979374599040582124)
XLA Ops:
  2.4 4.4 %collective-permute-start = (bf16[80,1024]{1,0:T(8,128)(2,1)}, bf16[80,1024]{1,0:T(8,128)(2,1)S(1)}, u32[]{:S(2)}, u32[]{:S(2)}) collective-permute-start(bf16[80,1024]{1,0:T(8,128)(2,1)} %get-tuple-element.32), channel_id=1, source_target_pairs={{0,0},{1,4},{2,2},{3,6},{4,1},{5,5},{6,3},{7,7},{8,8},{9,12},{10,1... | collective-permute-start | bytes 491528 | tf_op jit(solution)/shard_map/ppermute | solution.py:31
  6.9 5.6 %collective-permute-start.1 = (bf16[64,1024]{1,0:T(8,128)(2,1)}, bf16[64,1024]{1,0:T(8,128)(2,1)S(1)}, u32[]{:S(2)}, u32[]{:S(2)}) collective-permute-start(bf16[64,1024]{1,0:T(8,128)(2,1)} %get-tuple-element.33), channel_id=1, source_target_pairs={{8,0},{9,4},{10,2},{11,6},{12,1},{13,5},{14,3},{15,7},{16,8},{17,1... | collective-permute-start | bytes 393224 | tf_op jit(solution)/shard_map/ppermute | solution.py:31
  14.4 4.9 %shard_map.93 = bf16[32,264,128]{2,1,0:T(8,128)(2,1)} custom-call(s32[32]{0:T(128)} %bitcast.48, bf16[512,2,1024]{2,1,0:T(2,128)(2,1)} %bitcast.50), custom_call_target="tpu_custom_call" | custom-call | bytes 16777216 | tf_op jit(solution)/shard_map/pallas_call | solution.py:114
  19.4 10.4 %all-to-all-start = ((bf16[32,264,128]{2,1,0:T(8,128)(2,1)}), bf16[32,264,128]{2,1,0:T(8,128)(2,1)}, u32[]{:S(2)}, u32[]{:S(2)}) async-start(bf16[32,264,128]{2,1,0:T(8,128)(2,1)} %shard_map.93), calls=%async_computation | async-start | bytes 4325376 | tf_op jit(solution)/shard_map/all_to_all | solution.py:248
  32.6 2.6 %collective-permute-start.6 = (bf16[128,1024]{1,0:T(8,128)(2,1)S(1)}, bf16[128,1024]{1,0:T(8,128)(2,1)S(1)}, u32[]{:S(2)}, u32[]{:S(2)}) collective-permute-start(bf16[128,1024]{1,0:T(8,128)(2,1)S(1)} %pad_maximum_fusion.5), channel_id=1, source_target_pairs={{0,6},{1,7},{2,4},{3,5},{4,2},{5,3},{6,0},{7,1},{8,14},{9,15},{10,... | collective-permute-start | bytes 786440 | tf_op jit(solution)/shard_map/ppermute | solution.py:31
  35.3 10.9 %collective-permute-done.3 = bf16[128,1024]{1,0:T(8,128)(2,1)S(1)} collective-permute-done((bf16[128,1024]{1,0:T(8,128)(2,1)S(1)}, bf16[128,1024]{1,0:T(8,128)(2,1)S(1)}, u32[]{:S(2)}, u32[]{:S(2)}) %collective-permute-start.3) | collective-permute-done | bytes 262176 | tf_op jit(solution)/shard_map/ppermute | solution.py:31
  51.5 3.5 %fusion.7 = f32[256,1024]{1,0:T(8,128)S(1)} fusion(bf16[1024,2048]{1,0:T(8,128)(2,1)} %bitcast.59, bf16[128,1024]{1,0:T(8,128)(2,1)S(1)} %get-tuple-element.86, bf16[128,1024]{1,0:T(8,128)(2,1)S(1)} %get-tuple-element.87, bf16[128,1024]{1,0:T(8,128)(2,1)S(1)} %get-tuple-element.88, bf16[128,1024]{1,0:T(8,128)(2,1)S(1)} %get-tuple-element.85), kind=kOutput, calls=%fused_computation.6 | convolution fusion | flops 1077936128 | bytes 6291456 | tf_op jit(solution)/shard_map/dot_general | solution.py:266
  56.4 3.6 %collective-permute-done.13 = bf16[128,1024]{1,0:T(8,128)(2,1)S(1)} collective-permute-done((bf16[128,1024]{1,0:T(8,128)(2,1)S(1)}, bf16[128,1024]{1,0:T(8,128)(2,1)S(1)}, u32[]{:S(2)}, u32[]{:S(2)}) %collective-permute-start.13) | collective-permute-done | bytes 262176 | tf_op jit(solution)/shard_map/ppermute | solution.py:31
  60.0 3.4 %collective-permute-done.14 = bf16[128,1024]{1,0:T(8,128)(2,1)S(1)} collective-permute-done((bf16[128,1024]{1,0:T(8,128)(2,1)S(1)}, bf16[128,1024]{1,0:T(8,128)(2,1)S(1)}, u32[]{:S(2)}, u32[]{:S(2)}) %collective-permute-start.14) | collective-permute-done | bytes 262176 | tf_op jit(solution)/shard_map/ppermute | solution.py:31
  71.5 9.7 %all-to-all-done.kv_ref = bf16[32,264,128]{2,1,0:T(8,128)(2,1)} async-done(((bf16[32,264,128]{2,1,0:T(8,128)(2,1)}), bf16[32,264,128]{2,1,0:T(8,128)(2,1)}, u32[]{:S(2)}, u32[]{:S(2)}) %all-to-all-start) | async-done | bytes 2162720 | tf_op jit(solution)/shard_map/all_to_all | solution.py:248
  82.7 8.4 %shard_map.95 = (bf16[32,256,128]{2,1,0:T(8,128)(2,1)}, bf16[128,1024]{1,0:T(8,128)(2,1)}, bf16[128,1024]{1,0:T(8,128)(2,1)}) custom-call(s32[2]{0:T(128)} %fusion.18.count_ref, bf16[32,128]{1,0:T(8,128)(2,1)} %bitcast.58, bf16[128,1024]{1,0:T(8,128)(2,1)} %pad_maximum_fusion.4.query_ref, bf16[128,1024]{1,0:T(8,128)(2,1)} %add_convert_fusion.1.grad_ref, ...), custom_call_target="tpu_custom_call" | custom-call | flops 805306368 | bytes 5373952 | tf_op jit(solution)/shard_map/pallas_call | solution.py:205
  91.1 5.0 %all-to-all-start.1 = ((bf16[32,256,128]{2,1,0:T(8,128)(2,1)}), bf16[32,256,128]{2,1,0:T(8,128)(2,1)S(1)}, u32[]{:S(2)}, u32[]{:S(2)}) async-start(bf16[32,256,128]{2,1,0:T(8,128)(2,1)} %get-tuple-element.49), calls=%async_computation.1 | async-start | bytes 4194304 | tf_op jit(solution)/shard_map/all_to_all | solution.py:285
  96.2 4.0 %collective-permute-done.8 = bf16[128,1024]{1,0:T(8,128)(2,1)S(1)} collective-permute-done((bf16[128,1024]{1,0:T(8,128)(2,1)}, bf16[128,1024]{1,0:T(8,128)(2,1)S(1)}, u32[]{:S(2)}, u32[]{:S(2)}) %collective-permute-start.8) | collective-permute-done | bytes 262176 | tf_op jit(solution)/shard_map/ppermute | solution.py:31
  109.3 4.3 %collective-permute-start.11 = (bf16[512,512]{1,0:T(8,128)(2,1)S(1)}, bf16[512,512]{1,0:T(8,128)(2,1)S(1)}, u32[]{:S(2)}, u32[]{:S(2)}) collective-permute-start(bf16[512,512]{1,0:T(8,128)(2,1)S(1)} %pad_maximum_fusion.2), channel_id=1, source_target_pairs={{0,8},{1,9},{2,10},{3,11},{4,12},{5,13},{6,14},{7,15},{8,0},{9,1},... | collective-permute-start | bytes 1572872 | tf_op jit(solution)/shard_map/ppermute | solution.py:31
  115.2 2.7 %fusion.4 = bf16[512,1024]{1,0:T(8,128)(2,1)S(1)} fusion(bf16[1024,512]{1,0:T(8,128)(2,1)S(1)} %constant_dynamic-update-slice_fusion, bf16[512,1024]{1,0:T(8,128)(2,1)} %collective-permute-done.15, bf16[512,1024]{1,0:T(8,128)(2,1)S(1)} %copy-done.3), kind=kOutput, calls=%fused_computation.5 | convolution fusion | flops 1078460416 | bytes 4194304 | tf_op jit(solution)/shard_map/dot_general | solution.py:295
  120.5 2.9 %collective-permute-start.19 = (bf16[128,1024]{1,0:T(8,128)(2,1)S(1)}, bf16[128,1024]{1,0:T(8,128)(2,1)S(1)}, u32[]{:S(2)}, u32[]{:S(2)}) collective-permute-start(bf16[128,1024]{1,0:T(8,128)(2,1)S(1)} %get-tuple-element.78), channel_id=1, source_target_pairs={{0,4},{1,5},{2,6},{3,7},{4,0},{5,1},{6,2},{7,3},{8,12},{9,13},{10,... | collective-permute-start | bytes 786440 | tf_op jit(solution)/shard_map/ppermute | solution.py:31
  126.9 6.0 %collective-permute-start.26 = (bf16[64,1024]{1,0:T(8,128)(2,1)}, bf16[64,1024]{1,0:T(8,128)(2,1)S(1)}, u32[]{:S(2)}, u32[]{:S(2)}) collective-permute-start(bf16[64,1024]{1,0:T(8,128)(2,1)} %get-tuple-element.96), channel_id=1, source_target_pairs={{0,8},{1,9},{2,10},{3,11},{4,12},{5,13},{6,14},{7,15},{8,16},{9,17... | collective-permute-start | bytes 393224 | tf_op jit(solution)/shard_map/ppermute | solution.py:31
  137.4 11.6 %collective-permute-done.16 = bf16[4,4,16,512]{3,0,2,1:T(4,128)(2,1)S(1)} collective-permute-done((bf16[4,4,16,512]{3,0,2,1:T(4,128)(2,1)S(1)}, bf16[4,4,16,512]{3,0,2,1:T(4,128)(2,1)S(1)}, u32[]{:S(2)}, u32[]{:S(2)}) %collective-permute-start.16) | collective-permute-done | bytes 262176 | tf_op jit(solution)/shard_map/ppermute | solution.py:31
  151.3 3.2 %collective-permute-start.21 = (bf16[4,16,1024]{2,0,1:T(4,128)(2,1)S(1)}, bf16[4,16,1024]{2,0,1:T(4,128)(2,1)S(1)}, u32[]{:S(2)}, u32[]{:S(2)}) collective-permute-start(bf16[4,16,1024]{2,0,1:T(4,128)(2,1)S(1)} %get-tuple-element.89), channel_id=1, source_target_pairs={{0,128},{1,129},{2,130},{3,131},{4,132},{5,133},{6,134},{7,135},{8... | collective-permute-start | bytes 393224 | tf_op jit(solution)/shard_map/ppermute | solution.py:31
  158.1 4.5 %collective-permute-start.24 = (bf16[80,1024]{1,0:T(8,128)(2,1)S(1)}, bf16[80,1024]{1,0:T(8,128)(2,1)S(1)}, u32[]{:S(2)}, u32[]{:S(2)}) collective-permute-start(bf16[80,1024]{1,0:T(8,128)(2,1)S(1)} %pad_maximum_fusion.6), channel_id=1, source_target_pairs={{0,0},{1,4},{2,2},{3,6},{4,1},{5,5},{6,3},{7,7},{8,8},{9,12},{10,1... | collective-permute-start | bytes 491528 | tf_op jit(solution)/shard_map/ppermute | solution.py:31
  162.7 3.3 %shard_map.96 = bf16[512,2,1024]{2,1,0:T(2,128)(2,1)} custom-call(s32[32]{0:T(128)S(1)} %bitcast.49, bf16[32,256,128]{2,1,0:T(8,128)(2,1)S(1)} %all-to-all-done.1.part_ref), custom_call_target="tpu_custom_call" | custom-call | bytes 8388608 | tf_op jit(solution)/shard_map/pallas_call | solution.py:142
  165.9 6.1 %collective-permute-start.25 = (bf16[64,1024]{1,0:T(8,128)(2,1)S(1)}, bf16[64,1024]{1,0:T(8,128)(2,1)S(1)}, u32[]{:S(2)}, u32[]{:S(2)}) collective-permute-start(bf16[64,1024]{1,0:T(8,128)(2,1)S(1)} %get-tuple-element.98), channel_id=1, source_target_pairs={{0,8},{1,12},{2,10},{3,14},{4,9},{5,13},{6,11},{7,15},{8,16},{9,20... | collective-permute-start | bytes 393224 | tf_op jit(solution)/shard_map/ppermute | solution.py:31
  172.2 3.9 %collective-permute-done.25 = bf16[64,1024]{1,0:T(8,128)(2,1)S(1)} collective-permute-done((bf16[64,1024]{1,0:T(8,128)(2,1)S(1)}, bf16[64,1024]{1,0:T(8,128)(2,1)S(1)}, u32[]{:S(2)}, u32[]{:S(2)}) %collective-permute-start.25) | collective-permute-done | bytes 131104 | tf_op jit(solution)/shard_map/ppermute | solution.py:31
  176.1 2.6 %collective-permute-start.28 = (bf16[4,4,1024]{2,0,1:T(4,128)(2,1)S(1)}, bf16[4,4,1024]{2,0,1:T(4,128)(2,1)S(1)}, u32[]{:S(2)}, u32[]{:S(2)}) collective-permute-start(bf16[4,4,1024]{2,0,1:T(4,128)(2,1)S(1)} %select_bitcast_fusion.2), channel_id=1, source_target_pairs={{0,16},{1,17},{2,18},{3,19},{4,20},{5,21},{6,22},{7,23},{8,24},{9,... | collective-permute-start | bytes 98312 | tf_op jit(solution)/shard_map/ppermute | solution.py:31
  (110 shorter events, 56.5 us)
Async XLA Ops:
  2.4 16.9 %collective-permute-start = (bf16[80,1024]{1,0:T(8,128)(2,1)}, bf16[80,1024]{1,0:T(8,128)(2,1)S(1)}, u32[]{:S(2)}, u32[]{:S(2)}) collective-permute-start(bf16[80,1024]{1,0:T(8,128)(2,1)} %get-tuple-element.32), channel_id=1, source_target_pairs={{0,0},{1,4},{2,2},{3,6},{4,1},{5,5},{6,3},{7,7},{8,8},{9,12},{10,1... | collective-permute-start | bytes 491528 | tf_op jit(solution)/shard_map/ppermute | solution.py:31
  6.9 12.5 %collective-permute-start.1 = (bf16[64,1024]{1,0:T(8,128)(2,1)}, bf16[64,1024]{1,0:T(8,128)(2,1)S(1)}, u32[]{:S(2)}, u32[]{:S(2)}) collective-permute-start(bf16[64,1024]{1,0:T(8,128)(2,1)} %get-tuple-element.33), channel_id=1, source_target_pairs={{8,0},{9,4},{10,2},{11,6},{12,1},{13,5},{14,3},{15,7},{16,8},{17,1... | collective-permute-start | bytes 393224 | tf_op jit(solution)/shard_map/ppermute | solution.py:31
  19.4 61.9 %all-to-all-start = ((bf16[32,264,128]{2,1,0:T(8,128)(2,1)}), bf16[32,264,128]{2,1,0:T(8,128)(2,1)}, u32[]{:S(2)}, u32[]{:S(2)}) async-start(bf16[32,264,128]{2,1,0:T(8,128)(2,1)} %shard_map.93), calls=%async_computation | async-start | bytes 4325376 | tf_op jit(solution)/shard_map/all_to_all | solution.py:248
  30.0 16.3 %collective-permute-start.3 = (bf16[128,1024]{1,0:T(8,128)(2,1)S(1)}, bf16[128,1024]{1,0:T(8,128)(2,1)S(1)}, u32[]{:S(2)}, u32[]{:S(2)}) collective-permute-start(bf16[128,1024]{1,0:T(8,128)(2,1)S(1)} %pad_maximum_fusion.5), channel_id=1, source_target_pairs={{0,16},{1,17},{2,18},{3,19},{4,20},{5,21},{6,22},{7,23},{8,24},{9,... | collective-permute-start | bytes 786440 | tf_op jit(solution)/shard_map/ppermute | solution.py:31
  31.4 14.8 %collective-permute-start.4 = (bf16[128,1024]{1,0:T(8,128)(2,1)S(1)}, bf16[128,1024]{1,0:T(8,128)(2,1)S(1)}, u32[]{:S(2)}, u32[]{:S(2)}) collective-permute-start(bf16[128,1024]{1,0:T(8,128)(2,1)S(1)} %pad_maximum_fusion.5), channel_id=1, source_target_pairs={{0,2},{1,3},{2,0},{3,1},{4,6},{5,7},{6,4},{7,5},{8,10},{9,11},{10,... | collective-permute-start | bytes 786440 | tf_op jit(solution)/shard_map/ppermute | solution.py:31
  32.6 13.6 %collective-permute-start.5 = (bf16[128,1024]{1,0:T(8,128)(2,1)S(1)}, bf16[128,1024]{1,0:T(8,128)(2,1)S(1)}, u32[]{:S(2)}, u32[]{:S(2)}) collective-permute-start(bf16[128,1024]{1,0:T(8,128)(2,1)S(1)} %pad_maximum_fusion.5), channel_id=1, source_target_pairs={{0,4},{1,5},{2,6},{3,7},{4,0},{5,1},{6,2},{7,3},{8,12},{9,13},{10,... | collective-permute-start | bytes 786440 | tf_op jit(solution)/shard_map/ppermute | solution.py:31
  32.6 14.8 %collective-permute-start.6 = (bf16[128,1024]{1,0:T(8,128)(2,1)S(1)}, bf16[128,1024]{1,0:T(8,128)(2,1)S(1)}, u32[]{:S(2)}, u32[]{:S(2)}) collective-permute-start(bf16[128,1024]{1,0:T(8,128)(2,1)S(1)} %pad_maximum_fusion.5), channel_id=1, source_target_pairs={{0,6},{1,7},{2,4},{3,5},{4,2},{5,3},{6,0},{7,1},{8,14},{9,15},{10,... | collective-permute-start | bytes 786440 | tf_op jit(solution)/shard_map/ppermute | solution.py:31
  47.5 8.9 %collective-permute-start.12 = (bf16[128,1024]{1,0:T(8,128)(2,1)S(1)}, bf16[128,1024]{1,0:T(8,128)(2,1)S(1)}, u32[]{:S(2)}, u32[]{:S(2)}) collective-permute-start(bf16[128,1024]{1,0:T(8,128)(2,1)S(1)} %collective-permute-done.3), channel_id=1, source_target_pairs={{0,2},{1,3},{2,0},{3,1},{4,6},{5,7},{6,4},{7,5},{8,10},{9,11},{10,... | collective-permute-start | bytes 786440 | tf_op jit(solution)/shard_map/ppermute | solution.py:31
  47.5 12.5 %collective-permute-start.13 = (bf16[128,1024]{1,0:T(8,128)(2,1)S(1)}, bf16[128,1024]{1,0:T(8,128)(2,1)S(1)}, u32[]{:S(2)}, u32[]{:S(2)}) collective-permute-start(bf16[128,1024]{1,0:T(8,128)(2,1)S(1)} %collective-permute-done.3), channel_id=1, source_target_pairs={{0,4},{1,5},{2,6},{3,7},{4,0},{5,1},{6,2},{7,3},{8,12},{9,13},{10,... | collective-permute-start | bytes 786440 | tf_op jit(solution)/shard_map/ppermute | solution.py:31
  50.0 13.5 %collective-permute-start.14 = (bf16[128,1024]{1,0:T(8,128)(2,1)S(1)}, bf16[128,1024]{1,0:T(8,128)(2,1)S(1)}, u32[]{:S(2)}, u32[]{:S(2)}) collective-permute-start(bf16[128,1024]{1,0:T(8,128)(2,1)S(1)} %collective-permute-done.3), channel_id=1, source_target_pairs={{0,6},{1,7},{2,4},{3,5},{4,2},{5,3},{6,0},{7,1},{8,14},{9,15},{10,... | collective-permute-start | bytes 786440 | tf_op jit(solution)/shard_map/ppermute | solution.py:31
  55.0 15.7 %collective-permute-start.7 = (bf16[128,1024]{1,0:T(8,128)(2,1)S(1)}, bf16[128,1024]{1,0:T(8,128)(2,1)S(1)}, u32[]{:S(2)}, u32[]{:S(2)}) collective-permute-start(bf16[128,1024]{1,0:T(8,128)(2,1)S(1)} %select_convert_fusion), channel_id=1, source_target_pairs={{0,1},{1,0},{2,3},{3,2},{4,5},{5,4},{6,7},{7,6},{8,9},{9,8},{10,11... | collective-permute-start | bytes 786440 | tf_op jit(solution)/shard_map/ppermute | solution.py:31
  65.2 25.9 %collective-permute-start.15 = (bf16[512,1024]{1,0:T(8,128)(2,1)S(1)}, bf16[512,1024]{1,0:T(8,128)(2,1)}, u32[]{:S(2)}, u32[]{:S(2)}) collective-permute-start(bf16[512,1024]{1,0:T(8,128)(2,1)S(1)} %get-tuple-element.74), channel_id=1, source_target_pairs={{0,8},{1,9},{2,10},{3,11},{4,12},{5,13},{6,14},{7,15},{8,0},{9,1},... | collective-permute-start | bytes 3145736 | tf_op jit(solution)/shard_map/ppermute | solution.py:31
  91.1 9.1 %collective-permute-start.8 = (bf16[128,1024]{1,0:T(8,128)(2,1)}, bf16[128,1024]{1,0:T(8,128)(2,1)S(1)}, u32[]{:S(2)}, u32[]{:S(2)}) collective-permute-start(bf16[128,1024]{1,0:T(8,128)(2,1)} %get-tuple-element.43), channel_id=1, source_target_pairs={{0,1},{1,0},{2,3},{3,2},{4,5},{5,4},{6,7},{7,6},{8,9},{9,8},{10,11... | collective-permute-start | bytes 786440 | tf_op jit(solution)/shard_map/ppermute | solution.py:31
  91.1 60.0 %all-to-all-start.1 = ((bf16[32,256,128]{2,1,0:T(8,128)(2,1)}), bf16[32,256,128]{2,1,0:T(8,128)(2,1)S(1)}, u32[]{:S(2)}, u32[]{:S(2)}) async-start(bf16[32,256,128]{2,1,0:T(8,128)(2,1)} %get-tuple-element.49), calls=%async_computation.1 | async-start | bytes 4194304 | tf_op jit(solution)/shard_map/all_to_all | solution.py:285
  120.5 14.6 %collective-permute-start.19 = (bf16[128,1024]{1,0:T(8,128)(2,1)S(1)}, bf16[128,1024]{1,0:T(8,128)(2,1)S(1)}, u32[]{:S(2)}, u32[]{:S(2)}) collective-permute-start(bf16[128,1024]{1,0:T(8,128)(2,1)S(1)} %get-tuple-element.78), channel_id=1, source_target_pairs={{0,4},{1,5},{2,6},{3,7},{4,0},{5,1},{6,2},{7,3},{8,12},{9,13},{10,... | collective-permute-start | bytes 786440 | tf_op jit(solution)/shard_map/ppermute | solution.py:31
  123.4 13.7 %collective-permute-start.20 = (bf16[128,1024]{1,0:T(8,128)(2,1)S(1)}, bf16[128,1024]{1,0:T(8,128)(2,1)S(1)}, u32[]{:S(2)}, u32[]{:S(2)}) collective-permute-start(bf16[128,1024]{1,0:T(8,128)(2,1)S(1)} %get-tuple-element.77), channel_id=1, source_target_pairs={{0,6},{1,7},{2,4},{3,5},{4,2},{5,3},{6,0},{7,1},{8,14},{9,15},{10,... | collective-permute-start | bytes 786440 | tf_op jit(solution)/shard_map/ppermute | solution.py:31
  124.4 24.5 %collective-permute-start.16 = (bf16[4,4,16,512]{3,0,2,1:T(4,128)(2,1)S(1)}, bf16[4,4,16,512]{3,0,2,1:T(4,128)(2,1)S(1)}, u32[]{:S(2)}, u32[]{:S(2)}) collective-permute-start(bf16[4,4,16,512]{3,0,2,1:T(4,128)(2,1)S(1)} %get-tuple-element.92), channel_id=1, source_target_pairs={{0,32},{1,33},{2,34},{3,35},{4,36},{5,37},{6,38},{7,39},{8,40},{9,... | collective-permute-start | bytes 786440 | tf_op jit(solution)/shard_map/ppermute | solution.py:31
  126.9 23.4 %collective-permute-start.17 = (bf16[4,4,16,512]{3,0,2,1:T(4,128)(2,1)S(1)}, bf16[4,4,16,512]{3,0,2,1:T(4,128)(2,1)S(1)}, u32[]{:S(2)}, u32[]{:S(2)}) collective-permute-start(bf16[4,4,16,512]{3,0,2,1:T(4,128)(2,1)S(1)} %get-tuple-element.93), channel_id=1, source_target_pairs={{0,224},{1,225},{2,226},{3,227},{4,228},{5,229},{6,230},{7,231},{8... | collective-permute-start | bytes 786440 | tf_op jit(solution)/shard_map/ppermute | solution.py:31
  126.9 54.0 %collective-permute-start.26 = (bf16[64,1024]{1,0:T(8,128)(2,1)}, bf16[64,1024]{1,0:T(8,128)(2,1)S(1)}, u32[]{:S(2)}, u32[]{:S(2)}) collective-permute-start(bf16[64,1024]{1,0:T(8,128)(2,1)} %get-tuple-element.96), channel_id=1, source_target_pairs={{0,8},{1,9},{2,10},{3,11},{4,12},{5,13},{6,14},{7,15},{8,16},{9,17... | collective-permute-start | bytes 393224 | tf_op jit(solution)/shard_map/ppermute | solution.py:31
  151.3 14.6 %collective-permute-start.21 = (bf16[4,16,1024]{2,0,1:T(4,128)(2,1)S(1)}, bf16[4,16,1024]{2,0,1:T(4,128)(2,1)S(1)}, u32[]{:S(2)}, u32[]{:S(2)}) collective-permute-start(bf16[4,16,1024]{2,0,1:T(4,128)(2,1)S(1)} %get-tuple-element.89), channel_id=1, source_target_pairs={{0,128},{1,129},{2,130},{3,131},{4,132},{5,133},{6,134},{7,135},{8... | collective-permute-start | bytes 393224 | tf_op jit(solution)/shard_map/ppermute | solution.py:31
  154.5 17.6 %collective-permute-start.22 = (bf16[4,16,1024]{2,0,1:T(4,128)(2,1)S(1)}, bf16[4,16,1024]{2,0,1:T(4,128)(2,1)S(1)}, u32[]{:S(2)}, u32[]{:S(2)}) collective-permute-start(bf16[4,16,1024]{2,0,1:T(4,128)(2,1)S(1)} %get-tuple-element.91), channel_id=1, source_target_pairs={{0,64},{1,65},{2,66},{3,67},{4,68},{5,69},{6,70},{7,71},{8,72},{9,... | collective-permute-start | bytes 393224 | tf_op jit(solution)/shard_map/ppermute | solution.py:31
  155.5 16.6 %collective-permute-start.23 = (bf16[4,16,1024]{2,0,1:T(4,128)(2,1)S(1)}, bf16[4,16,1024]{2,0,1:T(4,128)(2,1)S(1)}, u32[]{:S(2)}, u32[]{:S(2)}) collective-permute-start(bf16[4,16,1024]{2,0,1:T(4,128)(2,1)S(1)} %get-tuple-element.90), channel_id=1, source_target_pairs={{0,192},{1,193},{2,194},{3,195},{4,196},{5,197},{6,198},{7,199},{8... | collective-permute-start | bytes 393224 | tf_op jit(solution)/shard_map/ppermute | solution.py:31
  158.1 18.0 %collective-permute-start.24 = (bf16[80,1024]{1,0:T(8,128)(2,1)S(1)}, bf16[80,1024]{1,0:T(8,128)(2,1)S(1)}, u32[]{:S(2)}, u32[]{:S(2)}) collective-permute-start(bf16[80,1024]{1,0:T(8,128)(2,1)S(1)} %pad_maximum_fusion.6), channel_id=1, source_target_pairs={{0,0},{1,4},{2,2},{3,6},{4,1},{5,5},{6,3},{7,7},{8,8},{9,12},{10,1... | collective-permute-start | bytes 491528 | tf_op jit(solution)/shard_map/ppermute | solution.py:31
  165.9 10.2 %collective-permute-start.25 = (bf16[64,1024]{1,0:T(8,128)(2,1)S(1)}, bf16[64,1024]{1,0:T(8,128)(2,1)S(1)}, u32[]{:S(2)}, u32[]{:S(2)}) collective-permute-start(bf16[64,1024]{1,0:T(8,128)(2,1)S(1)} %get-tuple-element.98), channel_id=1, source_target_pairs={{0,8},{1,12},{2,10},{3,14},{4,9},{5,13},{6,11},{7,15},{8,16},{9,20... | collective-permute-start | bytes 393224 | tf_op jit(solution)/shard_map/ppermute | solution.py:31
  (16 other events, 186.0 us)
